TPU v7x, 32 devices: a whole 2x2x4 slice. The times are simulated.
32 devices in a mesh: section: 4 (over y, x), tok: 8 (over z, core).
Axes of the slice: x: 2, y: 2, z: 4, core: 2. Of those that a mesh axis runs over, the one named last changes fastest.
Arguments:
- tokens: bfloat16 [2, 1024, 768], P(None, 'tok'), may hold values from -6 to 6
- cotangent: bfloat16 [2, 1024, 768], P(None, 'tok'), may hold values from -0.13183594 to 0.13183594
- window_slot: int32 [1024], P('tok'), may hold values from 0 to 1023, as said below
- slot_token: int32 [1024], P('tok'), may hold values from 0 to 1023, as said below
- norm_gain: float32 [4, 768], P('section'), may hold values from 0.25 to 1.75
- qkv_weight: bfloat16 [4, 768, 2304], P('section')
- out_weight: bfloat16 [4, 768, 768], P('section'), may hold values from -0.21875 to 0.21875
Outputs:
- grad_qkv: float32 [4, 768, 2304], P('section', 'tok')
- grad_out: float32 [4, 768, 768], P('section', 'tok')
- grad_gain: float32 [4, 768], P('section', 'tok')
Inputs may be any that keep to these rules, and one draw needn't show every extreme that they name: window_slot and slot_token are inverse permutations: slot_token[window_slot[t]] = t. Slots k * 128 .. (k + 1) * 128 - 1 lie on the k-th device of tok, and the tokens of every device fill exactly 16 slots of every device. `slot_token`: the inverse permutation of window_slot.
All inputs are finite; a program needn't handle non-finite values.
Results may differ from a plain program's by a relative error of at most 0.025.
Values may be sent and summed in bfloat16 or wider, within the bound.
A program may use at most 128 MiB of HBM per device.

v0:
```python
import jax
import jax.numpy as jnp
from jax import lax
from jax.sharding import PartitionSpec as P

HEADS = 12
WINDOW = 32


EPSILON = 1e-06


def from_behind(value, axis, steps):
    count = lax.axis_size(axis)
    first, last = (max(0, -steps), min(count, count - steps))
    return lax.ppermute(value, axis, [(source, source + steps) for source in range(first, last)])


def normalize(rows_in, norm_scale):
    widened = rows_in.astype(jnp.float32)
    factor = lax.rsqrt(jnp.mean(widened * widened, axis=-1, keepdims=True) + EPSILON)
    return ((widened * factor * norm_scale).astype(jnp.bfloat16), factor)


def window_split(window_rows):
    row_total = window_rows.shape[0]
    head_dim = window_rows.shape[1] // 3 // HEADS
    shaped = window_rows.reshape(row_total // WINDOW, WINDOW, 3, HEADS, head_dim)
    return (shaped[:, :, 0], shaped[:, :, 1], shaped[:, :, 2], head_dim)


def window_soft(queries, key_rows, head_dim):
    scores = jnp.einsum(
        "wqhd,wkhd->whqk", queries, key_rows, preferred_element_type=jnp.float32
    ) * head_dim ** (-0.5)
    return jax.nn.softmax(scores, axis=-1)


def window_forward(window_rows):
    queries, key_rows, values, head_dim = window_split(window_rows)
    soft_weights = window_soft(queries, key_rows, head_dim).astype(jnp.bfloat16)
    mixed_rows = jnp.einsum(
        "whqk,wkhd->wqhd", soft_weights, values, preferred_element_type=jnp.float32
    )
    return mixed_rows.reshape(window_rows.shape[0], -1).astype(jnp.bfloat16)


def window_backward(window_rows, grad_rows):
    queries, key_rows, values, head_dim = window_split(window_rows)
    row_total = window_rows.shape[0]
    grad_mixed = grad_rows.reshape(row_total // WINDOW, WINDOW, HEADS, head_dim)
    soft_weights = window_soft(queries, key_rows, head_dim)
    soft_low = soft_weights.astype(jnp.bfloat16)
    grad_soft = jnp.einsum(
        "wqhd,wkhd->whqk", grad_mixed, values, preferred_element_type=jnp.float32
    )
    grad_values = jnp.einsum(
        "whqk,wqhd->wkhd", soft_low, grad_mixed, preferred_element_type=jnp.float32
    )
    grad_scores = soft_weights * (
        grad_soft - jnp.sum(soft_weights * grad_soft, axis=-1, keepdims=True)
    )
    grad_low = grad_scores.astype(jnp.bfloat16)
    temper = head_dim ** (-0.5)
    grad_queries = (
        jnp.einsum("whqk,wkhd->wqhd", grad_low, key_rows, preferred_element_type=jnp.float32)
        * temper
    )
    grad_keys = (
        jnp.einsum("whqk,wqhd->wkhd", grad_low, queries, preferred_element_type=jnp.float32)
        * temper
    )
    stacked = jnp.stack([grad_queries, grad_keys, grad_values], axis=2)
    return stacked.reshape(row_total, -1).astype(jnp.bfloat16)


def stored_update(stored, position, active, update):
    former = lax.dynamic_index_in_dim(stored, position, 0, keepdims=False)
    return lax.dynamic_update_index_in_dim(stored, jnp.where(active, update, former), position, 0)


def per_device(tokens, cotangent, window_slot, slot_token, norm_gain, qkv_weight, out_weight):
    micro_count, row_count, feature_width = tokens.shape
    section_count = lax.axis_size("section")
    section_index = lax.axis_index("section")
    norm_scale = norm_gain[0]
    qkv_matrix = qkv_weight[0]
    out_matrix = out_weight[0]
    target_device = window_slot // row_count
    send_order = jnp.argsort(target_device, stable=True)
    home_place = jnp.argsort(send_order)
    back_order = jnp.argsort(slot_token)
    slot_place = jnp.argsort(back_order)

    def pack_home(rows_in):
        return jnp.take(rows_in, send_order, axis=0)

    def place_home(rows_in):
        return jnp.take(rows_in, home_place, axis=0)

    def pack_window(rows_in):
        return jnp.take(rows_in, back_order, axis=0)

    def place_window(rows_in):
        return jnp.take(rows_in, slot_place, axis=0)

    steps_total = micro_count + section_count - 1
    zero_rows = jnp.zeros((micro_count, row_count, feature_width), jnp.bfloat16)
    start_carry = (
        jnp.zeros((row_count, feature_width), jnp.bfloat16),
        zero_rows,
        zero_rows,
        zero_rows,
        jnp.zeros((micro_count, row_count, 3 * feature_width), jnp.bfloat16),
    )

    def forward_step(step_index, carried):
        inflow, kept_input, kept_normed, kept_mixed, kept_window = carried
        micro_index = step_index - section_index
        active = (micro_index >= 0) & (micro_index < micro_count)
        clipped = jnp.clip(micro_index, 0, micro_count - 1)
        entering = lax.dynamic_index_in_dim(
            tokens, jnp.clip(step_index, 0, micro_count - 1), 0, keepdims=False
        )
        layer_in = jnp.where(section_index == 0, entering, inflow)
        normed = normalize(layer_in, norm_scale)[0]
        projected = jnp.dot(normed, qkv_matrix, preferred_element_type=jnp.float32).astype(
            jnp.bfloat16
        )
        window_rows = place_window(
            lax.all_to_all(pack_home(projected), "tok", split_axis=0, concat_axis=0, tiled=True)
        )
        mixed_window = window_forward(window_rows)
        mixed_rows = place_home(
            lax.all_to_all(
                pack_window(mixed_window), "tok", split_axis=0, concat_axis=0, tiled=True
            )
        )
        layer_out = (
            layer_in.astype(jnp.float32)
            + jnp.dot(mixed_rows, out_matrix, preferred_element_type=jnp.float32)
        ).astype(jnp.bfloat16)
        kept_input = stored_update(kept_input, clipped, active, layer_in)
        kept_normed = stored_update(kept_normed, clipped, active, normed)
        kept_mixed = stored_update(kept_mixed, clipped, active, mixed_rows)
        kept_window = stored_update(kept_window, clipped, active, window_rows)
        outflow = from_behind(layer_out, "section", 1)
        return (outflow, kept_input, kept_normed, kept_mixed, kept_window)

    leftover, kept_input, kept_normed, kept_mixed, kept_window = lax.fori_loop(
        0, steps_total, forward_step, start_carry
    )

    def backward_step(step_index, carried):
        inflow, qkv_total, out_total, scale_total = carried
        micro_index = step_index - (section_count - 1 - section_index)
        active = (micro_index >= 0) & (micro_index < micro_count)
        weight_on = active.astype(jnp.float32)
        clipped = jnp.clip(micro_index, 0, micro_count - 1)
        arriving = lax.dynamic_index_in_dim(
            cotangent, jnp.clip(step_index, 0, micro_count - 1), 0, keepdims=False
        )
        grad_layer = jnp.where(section_index == section_count - 1, arriving, inflow)
        layer_in = lax.dynamic_index_in_dim(kept_input, clipped, 0, keepdims=False)
        kept_rows = lax.dynamic_index_in_dim(kept_normed, clipped, 0, keepdims=False)
        mixed_rows = lax.dynamic_index_in_dim(kept_mixed, clipped, 0, keepdims=False)
        window_rows = lax.dynamic_index_in_dim(kept_window, clipped, 0, keepdims=False)
        out_total = out_total + weight_on * jnp.einsum(
            "td,te->de", mixed_rows, grad_layer, preferred_element_type=jnp.float32
        )
        grad_mixed = jnp.einsum(
            "te,de->td", grad_layer, out_matrix, preferred_element_type=jnp.float32
        ).astype(jnp.bfloat16)
        grad_arrived = lax.all_to_all(
            pack_home(grad_mixed), "tok", split_axis=0, concat_axis=0, tiled=True
        )
        grad_window = window_backward(window_rows, place_window(grad_arrived))
        grad_proj = place_home(
            lax.all_to_all(pack_window(grad_window), "tok", split_axis=0, concat_axis=0, tiled=True)
        )
        qkv_total = qkv_total + weight_on * jnp.einsum(
            "td,tc->dc", kept_rows, grad_proj, preferred_element_type=jnp.float32
        )
        grad_normed = jnp.einsum(
            "tc,dc->td", grad_proj, qkv_matrix, preferred_element_type=jnp.float32
        )
        widened = layer_in.astype(jnp.float32)
        factor = lax.rsqrt(jnp.mean(widened * widened, axis=-1, keepdims=True) + EPSILON)
        scale_total = scale_total + weight_on * jnp.sum(grad_normed * widened * factor, axis=0)
        scaled = norm_scale * grad_normed
        inner_mean = jnp.mean(scaled * widened, axis=-1, keepdims=True)
        grad_input = (
            grad_layer.astype(jnp.float32) + factor * scaled - widened * factor**3 * inner_mean
        ).astype(jnp.bfloat16)
        outflow = from_behind(grad_input, "section", -1)
        return (outflow, qkv_total, out_total, scale_total)

    back_carry = (
        jnp.zeros((row_count, feature_width), jnp.bfloat16),
        jnp.zeros(qkv_matrix.shape, jnp.float32),
        jnp.zeros(out_matrix.shape, jnp.float32),
        jnp.zeros(norm_scale.shape, jnp.float32),
    )
    leftover_grad, qkv_total, out_total, scale_total = lax.fori_loop(
        0, steps_total, backward_step, back_carry
    )
    qkv_share, out_share, scale_share = (
        lax.psum_scatter(qkv_total, "tok", scatter_dimension=0, tiled=True),
        lax.psum_scatter(out_total, "tok", scatter_dimension=0, tiled=True),
        lax.psum_scatter(scale_total, "tok", scatter_dimension=0, tiled=True),
    )
    return (qkv_share[None], out_share[None], scale_share[None])


def solution(mesh):
    placed = (
        P(None, "tok", None),
        P(None, "tok", None),
        P("tok"),
        P("tok"),
        P("section", None),
        P("section", None, None),
        P("section", None, None),
    )
    return jax.shard_map(
        per_device,
        mesh=mesh,
        in_specs=placed,
        out_specs=(P("section", "tok", None), P("section", "tok", None), P("section", "tok")),
        check_vma=False,
    )
```

profile of v0, /device:TPU:1, one launch (start us, length us, event | category | flops | bytes accessed | tf_op | source)
XLA Modules:
  0.0 751.9 jit_solution(2852541501307405902)
XLA Ops:
  13.1 3.2 sort.63
  21.5 304.5 %while.44 = (s32[]{:T(128)}, bf16[128,768]{1,0:T(8,128)(2,1)S(1)}, bf16[2,128,768]{2,1,0:T(8,128)(2,1)}, bf16[2,128,768]{2,1,0:T(8,128)(2,1)S(1)}, bf16[2,128,76...) while((s32[]{:T(128)}, bf16[128,768]{1,0:T(8,128)(2,1)S(1)}, ...), condition=%wide.region_8.11_spmd, body=%wide.region_4.10_spmd.sunk | while | flops 626550976 | bytes 34463832 | solution.py:150
  29.1 6.4 all-to-all-start
  37.3 14.0 %all-to-all-done = bf16[8,16,2304]{2,1,0:T(8,128)(2,1)S(1)} async-done(((bf16[8,16,2304]{2,1,0:T(8,128)(2,1)}), bf16[8,16,2304]{2,1,0:T(8,128)(2,1)S(1)}, u32[]{:S(2)}, u32[]{:S(2)}) %all-to-all-start) | async-done | bytes 589856 | tf_op jit(solution)/shard_map/while/body/eval_jaxpr/all_to_all | solution.py:131
  63.6 4.2 all-to-all-start.1
  68.0 6.3 all-to-all-done.1
  75.5 3.1 collective-permute-start
  84.2 2.7 convolution_convert_fusion.6
  88.8 6.5 all-to-all-start
  97.1 14.0 %all-to-all-done = bf16[8,16,2304]{2,1,0:T(8,128)(2,1)S(1)} async-done(((bf16[8,16,2304]{2,1,0:T(8,128)(2,1)}), bf16[8,16,2304]{2,1,0:T(8,128)(2,1)S(1)}, u32[]{:S(2)}, u32[]{:S(2)}) %all-to-all-start) | async-done | bytes 589856 | tf_op jit(solution)/shard_map/while/body/eval_jaxpr/all_to_all | solution.py:131
  123.4 4.2 all-to-all-start.1
  127.7 6.3 all-to-all-done.1
  135.3 4.1 collective-permute-start
  145.0 2.7 convolution_convert_fusion.6
  149.6 6.5 all-to-all-start
  157.9 14.0 %all-to-all-done = bf16[8,16,2304]{2,1,0:T(8,128)(2,1)S(1)} async-done(((bf16[8,16,2304]{2,1,0:T(8,128)(2,1)}), bf16[8,16,2304]{2,1,0:T(8,128)(2,1)S(1)}, u32[]{:S(2)}, u32[]{:S(2)}) %all-to-all-start) | async-done | bytes 589856 | tf_op jit(solution)/shard_map/while/body/eval_jaxpr/all_to_all | solution.py:131
  184.2 4.2 all-to-all-start.1
  188.5 6.3 all-to-all-done.1
  196.1 4.1 collective-permute-start
  205.7 2.7 convolution_convert_fusion.6
  210.3 6.5 all-to-all-start
  218.7 14.0 %all-to-all-done = bf16[8,16,2304]{2,1,0:T(8,128)(2,1)S(1)} async-done(((bf16[8,16,2304]{2,1,0:T(8,128)(2,1)}), bf16[8,16,2304]{2,1,0:T(8,128)(2,1)S(1)}, u32[]{:S(2)}, u32[]{:S(2)}) %all-to-all-start) | async-done | bytes 589856 | tf_op jit(solution)/shard_map/while/body/eval_jaxpr/all_to_all | solution.py:131
  245.0 4.2 all-to-all-start.1
  249.3 6.3 all-to-all-done.1
  256.8 4.9 collective-permute-start
  271.9 6.5 all-to-all-start
  280.2 14.0 %all-to-all-done = bf16[8,16,2304]{2,1,0:T(8,128)(2,1)S(1)} async-done(((bf16[8,16,2304]{2,1,0:T(8,128)(2,1)}), bf16[8,16,2304]{2,1,0:T(8,128)(2,1)S(1)}, u32[]{:S(2)}, u32[]{:S(2)}) %all-to-all-start) | async-done | bytes 589856 | tf_op jit(solution)/shard_map/while/body/eval_jaxpr/all_to_all | solution.py:131
  306.5 4.2 all-to-all-start.1
  310.9 6.3 all-to-all-done.1
  318.4 5.0 collective-permute-start
  326.7 300.5 %while.45 = (s32[]{:T(128)}, bf16[128,768]{1,0:T(8,128)(2,1)}, f32[768,2304]{1,0:T(8,128)}, f32[768,768]{1,0:T(8,128)}, f32[768]{0:T(1024)}, /*index=5*/pred[]{:...) while((s32[]{:T(128)}, bf16[128,768]{1,0:T(8,128)(2,1)}, ...), condition=%wide.region_16.19_spmd.clone, body=%wide.region_9.18_spmd.clone.sunk | while | flops 1251320704 | bytes 59212128 | solution.py:204
  330.8 6.5 all-to-all-start.2
  352.3 5.1 all-to-all-start.3
  359.5 13.9 %all-to-all-done.3 = bf16[8,16,2304]{2,1,0:T(8,128)(2,1)S(1)} async-done(((bf16[8,16,2304]{2,1,0:T(8,128)(2,1)}), bf16[8,16,2304]{2,1,0:T(8,128)(2,1)S(1)}, u32[]{:S(2)}, u32[]{:S(2)}) %all-to-all-start.3) | async-done | bytes 589856 | tf_op jit(solution)/shard_map/while/body/eval_jaxpr/all_to_all | solution.py:179
  374.3 3.5 fusion.108
  380.3 4.1 select_add_fusion.6
  384.4 4.1 collective-permute-done.1
  392.5 4.8 all-to-all-start.2
  412.3 5.1 all-to-all-start.3
  417.5 3.6 select_add_fusion.7
  421.2 12.2 %all-to-all-done.3 = bf16[8,16,2304]{2,1,0:T(8,128)(2,1)S(1)} async-done(((bf16[8,16,2304]{2,1,0:T(8,128)(2,1)}), bf16[8,16,2304]{2,1,0:T(8,128)(2,1)S(1)}, u32[]{:S(2)}, u32[]{:S(2)}) %all-to-all-start.3) | async-done | bytes 589856 | tf_op jit(solution)/shard_map/while/body/eval_jaxpr/all_to_all | solution.py:179
  434.3 3.5 fusion.108
  440.3 7.1 select_add_fusion.6
  452.5 4.8 all-to-all-start.2
  472.4 5.1 all-to-all-start.3
  477.6 3.6 select_add_fusion.7
  481.2 12.2 %all-to-all-done.3 = bf16[8,16,2304]{2,1,0:T(8,128)(2,1)S(1)} async-done(((bf16[8,16,2304]{2,1,0:T(8,128)(2,1)}), bf16[8,16,2304]{2,1,0:T(8,128)(2,1)S(1)}, u32[]{:S(2)}, u32[]{:S(2)}) %all-to-all-start.3) | async-done | bytes 589856 | tf_op jit(solution)/shard_map/while/body/eval_jaxpr/all_to_all | solution.py:179
  494.4 3.5 fusion.108
  500.3 7.1 select_add_fusion.6
  512.1 4.8 all-to-all-start.2
  531.9 5.1 all-to-all-start.3
  537.1 3.6 select_add_fusion.7
  540.8 12.2 %all-to-all-done.3 = bf16[8,16,2304]{2,1,0:T(8,128)(2,1)S(1)} async-done(((bf16[8,16,2304]{2,1,0:T(8,128)(2,1)}), bf16[8,16,2304]{2,1,0:T(8,128)(2,1)S(1)}, u32[]{:S(2)}, u32[]{:S(2)}) %all-to-all-start.3) | async-done | bytes 589856 | tf_op jit(solution)/shard_map/while/body/eval_jaxpr/all_to_all | solution.py:179
  554.0 3.5 fusion.108
  559.9 7.1 select_add_fusion.6
  571.7 4.8 all-to-all-start.2
  591.5 5.1 all-to-all-start.3
  596.7 3.6 select_add_fusion.7
  600.4 12.2 %all-to-all-done.3 = bf16[8,16,2304]{2,1,0:T(8,128)(2,1)S(1)} async-done(((bf16[8,16,2304]{2,1,0:T(8,128)(2,1)}), bf16[8,16,2304]{2,1,0:T(8,128)(2,1)S(1)}, u32[]{:S(2)}, u32[]{:S(2)}) %all-to-all-start.3) | async-done | bytes 589856 | tf_op jit(solution)/shard_map/while/body/eval_jaxpr/all_to_all | solution.py:179
  613.5 3.5 fusion.108
  619.5 7.1 select_add_fusion.6
  629.3 14.6 %all-reduce = f32[768]{0:T(1024)S(1)} all-reduce(f32[768]{0:T(1024)S(1)} %copy-done.18), channel_id=4, replica_groups=mesh['section'=4,'tok'=8] {'tok'}, use_global_device_ids=true, to_apply=%region_19.22.clone | all-reduce | flops 768 | bytes 6144
  644.5 20.7 %reduce-scatter.5.cloned.1.call-done = f32[96,768]{1,0:T(8,128)} async-done(((f32[768,768]{1,0:T(8,128)}), f32[96,768]{1,0:T(8,128)}) %reduce-scatter.5.cloned.1.call-update) | async-done | bytes 294928 | tf_op jit(solution)/shard_map/reduce_scatter | solution.py:209
  665.2 79.9 %reduce-scatter.3.cloned.1.call-done = f32[96,2304]{1,0:T(8,128)} async-done(((f32[768,2304]{1,0:T(8,128)}), f32[96,2304]{1,0:T(8,128)}) %reduce-scatter.3.cloned.1.call-update) | async-done | bytes 884752 | tf_op jit(solution)/shard_map/reduce_scatter | solution.py:208
  (633 shorter events, 249.9 us)
Async XLA Ops:
  7.2 14.3 %copy-start = (bf16[1,768,768]{2,1,0:T(8,128)(2,1)S(1)}, bf16[1,768,768]{2,1,0:T(8,128)(2,1)}, u32[]{:S(2)}) copy-start(bf16[1,768,768]{2,1,0:T(8,128)(2,1)} %param.21) | copy-start | bytes 3538948
  7.2 14.3 %copy-start.15 = (f32[1,768]{1,0:T(1,128)S(1)}, f32[1,768]{1,0:T(1,128)}, u32[]{:S(2)}) copy-start(f32[1,768]{1,0:T(1,128)} %param.19) | copy-start | bytes 9220
  7.2 658.0 %reduce-scatter.5.cloned.1.call-start = ((), (), s32[]{:S(2)}) async-start(), calls=%async_computation.7 | async-start | bytes 2654208 | tf_op jit(solution)/shard_map/reduce_scatter | solution.py:209
  21.5 15.8 %copy-start.6 = (bf16[2,128,768]{2,1,0:T(8,128)(2,1)}, bf16[2,128,768]{2,1,0:T(8,128)(2,1)S(1)}, u32[]{:S(2)}) copy-start(bf16[2,128,768]{2,1,0:T(8,128)(2,1)S(1)} %get-tuple-element.1192) | copy-start | bytes 1179652 | tf_op jit(solution)/shard_map/while
  29.1 22.3 %all-to-all-start = ((bf16[8,16,2304]{2,1,0:T(8,128)(2,1)}), bf16[8,16,2304]{2,1,0:T(8,128)(2,1)S(1)}, u32[]{:S(2)}, u32[]{:S(2)}) async-start(bf16[8,16,2304]{2,1,0:T(8,128)(2,1)} %bitcast.183), calls=%async_computation | async-start | bytes 1179648 | tf_op jit(solution)/shard_map/while/body/eval_jaxpr/all_to_all | solution.py:131
  60.4 7.4 copy-start.7
  60.4 7.4 copy-start.10
  63.6 10.6 %all-to-all-start.1 = ((bf16[8,16,768]{2,1,0:T(8,128)(2,1)}), bf16[8,16,768]{2,1,0:T(8,128)(2,1)S(1)}, u32[]{:S(2)}, u32[]{:S(2)}) async-start(bf16[8,16,768]{2,1,0:T(8,128)(2,1)} %bitcast.185), calls=%async_computation.1 | async-start | bytes 393216 | tf_op jit(solution)/shard_map/while/body/eval_jaxpr/all_to_all | solution.py:135
  75.5 5.7 collective-permute-start
  81.2 15.9 %copy-start.6 = (bf16[2,128,768]{2,1,0:T(8,128)(2,1)}, bf16[2,128,768]{2,1,0:T(8,128)(2,1)S(1)}, u32[]{:S(2)}) copy-start(bf16[2,128,768]{2,1,0:T(8,128)(2,1)S(1)} %get-tuple-element.1192) | copy-start | bytes 1179652 | tf_op jit(solution)/shard_map/while
  88.8 22.4 %all-to-all-start = ((bf16[8,16,2304]{2,1,0:T(8,128)(2,1)}), bf16[8,16,2304]{2,1,0:T(8,128)(2,1)S(1)}, u32[]{:S(2)}, u32[]{:S(2)}) async-start(bf16[8,16,2304]{2,1,0:T(8,128)(2,1)} %bitcast.183), calls=%async_computation | async-start | bytes 1179648 | tf_op jit(solution)/shard_map/while/body/eval_jaxpr/all_to_all | solution.py:131
  120.2 7.4 copy-start.7
  120.2 7.4 copy-start.10
  123.4 10.6 %all-to-all-start.1 = ((bf16[8,16,768]{2,1,0:T(8,128)(2,1)}), bf16[8,16,768]{2,1,0:T(8,128)(2,1)S(1)}, u32[]{:S(2)}, u32[]{:S(2)}) async-start(bf16[8,16,768]{2,1,0:T(8,128)(2,1)} %bitcast.185), calls=%async_computation.1 | async-start | bytes 393216 | tf_op jit(solution)/shard_map/while/body/eval_jaxpr/all_to_all | solution.py:135
  135.3 6.7 collective-permute-start
  142.0 15.9 %copy-start.6 = (bf16[2,128,768]{2,1,0:T(8,128)(2,1)}, bf16[2,128,768]{2,1,0:T(8,128)(2,1)S(1)}, u32[]{:S(2)}) copy-start(bf16[2,128,768]{2,1,0:T(8,128)(2,1)S(1)} %get-tuple-element.1192) | copy-start | bytes 1179652 | tf_op jit(solution)/shard_map/while
  149.6 22.4 %all-to-all-start = ((bf16[8,16,2304]{2,1,0:T(8,128)(2,1)}), bf16[8,16,2304]{2,1,0:T(8,128)(2,1)S(1)}, u32[]{:S(2)}, u32[]{:S(2)}) async-start(bf16[8,16,2304]{2,1,0:T(8,128)(2,1)} %bitcast.183), calls=%async_computation | async-start | bytes 1179648 | tf_op jit(solution)/shard_map/while/body/eval_jaxpr/all_to_all | solution.py:131
  181.0 7.4 copy-start.7
  181.0 7.4 copy-start.10
  184.2 10.6 %all-to-all-start.1 = ((bf16[8,16,768]{2,1,0:T(8,128)(2,1)}), bf16[8,16,768]{2,1,0:T(8,128)(2,1)S(1)}, u32[]{:S(2)}, u32[]{:S(2)}) async-start(bf16[8,16,768]{2,1,0:T(8,128)(2,1)} %bitcast.185), calls=%async_computation.1 | async-start | bytes 393216 | tf_op jit(solution)/shard_map/while/body/eval_jaxpr/all_to_all | solution.py:135
  196.1 6.7 collective-permute-start
  202.8 15.9 %copy-start.6 = (bf16[2,128,768]{2,1,0:T(8,128)(2,1)}, bf16[2,128,768]{2,1,0:T(8,128)(2,1)S(1)}, u32[]{:S(2)}) copy-start(bf16[2,128,768]{2,1,0:T(8,128)(2,1)S(1)} %get-tuple-element.1192) | copy-start | bytes 1179652 | tf_op jit(solution)/shard_map/while
  210.3 22.4 %all-to-all-start = ((bf16[8,16,2304]{2,1,0:T(8,128)(2,1)}), bf16[8,16,2304]{2,1,0:T(8,128)(2,1)S(1)}, u32[]{:S(2)}, u32[]{:S(2)}) async-start(bf16[8,16,2304]{2,1,0:T(8,128)(2,1)} %bitcast.183), calls=%async_computation | async-start | bytes 1179648 | tf_op jit(solution)/shard_map/while/body/eval_jaxpr/all_to_all | solution.py:131
  241.8 7.4 copy-start.7
  241.8 7.4 copy-start.10
  245.0 10.6 %all-to-all-start.1 = ((bf16[8,16,768]{2,1,0:T(8,128)(2,1)}), bf16[8,16,768]{2,1,0:T(8,128)(2,1)S(1)}, u32[]{:S(2)}, u32[]{:S(2)}) async-start(bf16[8,16,768]{2,1,0:T(8,128)(2,1)} %bitcast.185), calls=%async_computation.1 | async-start | bytes 393216 | tf_op jit(solution)/shard_map/while/body/eval_jaxpr/all_to_all | solution.py:135
  256.8 7.5 %collective-permute-start = (bf16[128,768]{1,0:T(8,128)(2,1)S(1)}, bf16[128,768]{1,0:T(8,128)(2,1)S(1)}, u32[]{:S(2)}, u32[]{:S(2)}) collective-permute-start(bf16[128,768]{1,0:T(8,128)(2,1)S(1)} %fusion.91), channel_id=1, source_target_pairs={{0,8},{8,16},{16,24},{1,9},{9,17},{17,25},{2,10},{10,18},{18,26},{... | collective-permute-start | bytes 589832 | tf_op jit(solution)/shard_map/while/body/eval_jaxpr/ppermute | solution.py:16
  264.4 15.9 %copy-start.6 = (bf16[2,128,768]{2,1,0:T(8,128)(2,1)}, bf16[2,128,768]{2,1,0:T(8,128)(2,1)S(1)}, u32[]{:S(2)}) copy-start(bf16[2,128,768]{2,1,0:T(8,128)(2,1)S(1)} %get-tuple-element.1192) | copy-start | bytes 1179652 | tf_op jit(solution)/shard_map/while
  271.9 22.4 %all-to-all-start = ((bf16[8,16,2304]{2,1,0:T(8,128)(2,1)}), bf16[8,16,2304]{2,1,0:T(8,128)(2,1)S(1)}, u32[]{:S(2)}, u32[]{:S(2)}) async-start(bf16[8,16,2304]{2,1,0:T(8,128)(2,1)} %bitcast.183), calls=%async_computation | async-start | bytes 1179648 | tf_op jit(solution)/shard_map/while/body/eval_jaxpr/all_to_all | solution.py:131
  303.3 7.4 copy-start.7
  303.4 7.4 copy-start.10
  306.5 10.6 %all-to-all-start.1 = ((bf16[8,16,768]{2,1,0:T(8,128)(2,1)}), bf16[8,16,768]{2,1,0:T(8,128)(2,1)S(1)}, u32[]{:S(2)}, u32[]{:S(2)}) async-start(bf16[8,16,768]{2,1,0:T(8,128)(2,1)} %bitcast.185), calls=%async_computation.1 | async-start | bytes 393216 | tf_op jit(solution)/shard_map/while/body/eval_jaxpr/all_to_all | solution.py:135
  318.4 7.6 %collective-permute-start = (bf16[128,768]{1,0:T(8,128)(2,1)S(1)}, bf16[128,768]{1,0:T(8,128)(2,1)S(1)}, u32[]{:S(2)}, u32[]{:S(2)}) collective-permute-start(bf16[128,768]{1,0:T(8,128)(2,1)S(1)} %fusion.91), channel_id=1, source_target_pairs={{0,8},{8,16},{16,24},{1,9},{9,17},{17,25},{2,10},{10,18},{18,26},{... | collective-permute-start | bytes 589832 | tf_op jit(solution)/shard_map/while/body/eval_jaxpr/ppermute | solution.py:16
  326.7 10.5 %copy-start.24 = (s32[128]{0:T(128)}, s32[128]{0:T(128)S(1)}, u32[]{:S(2)}) copy-start(s32[128]{0:T(128)S(1)} %get-tuple-element.1288) | copy-start | bytes 1540 | tf_op jit(solution)/shard_map/while
  327.5 9.8 %copy-start.1 = (bf16[2,128,2304]{2,1,0:T(8,128)(2,1)S(1)}, bf16[2,128,2304]{2,1,0:T(8,128)(2,1)}, u32[]{:S(2)}) copy-start(bf16[2,128,2304]{2,1,0:T(8,128)(2,1)} %get-tuple-element.1285) | copy-start | bytes 3538948 | tf_op jit(solution)/shard_map/while
  330.8 14.4 %all-to-all-start.2 = ((bf16[8,16,768]{2,1,0:T(8,128)(2,1)}), bf16[8,16,768]{2,1,0:T(8,128)(2,1)S(1)}, u32[]{:S(2)}, u32[]{:S(2)}) async-start(bf16[8,16,768]{2,1,0:T(8,128)(2,1)} %bitcast.207), calls=%async_computation.2 | async-start | bytes 393216 | tf_op jit(solution)/shard_map/while/body/eval_jaxpr/all_to_all | solution.py:174
  352.3 21.0 %all-to-all-start.3 = ((bf16[8,16,2304]{2,1,0:T(8,128)(2,1)}), bf16[8,16,2304]{2,1,0:T(8,128)(2,1)S(1)}, u32[]{:S(2)}, u32[]{:S(2)}) async-start(bf16[8,16,2304]{2,1,0:T(8,128)(2,1)} %bitcast.209), calls=%async_computation.3 | async-start | bytes 1179648 | tf_op jit(solution)/shard_map/while/body/eval_jaxpr/all_to_all | solution.py:179
  378.9 9.5 %collective-permute-start.1 = (bf16[128,768]{1,0:T(8,128)(2,1)S(1)}, bf16[128,768]{1,0:T(8,128)(2,1)}, u32[]{:S(2)}, u32[]{:S(2)}) collective-permute-start(bf16[128,768]{1,0:T(8,128)(2,1)S(1)} %fusion.109), channel_id=1, source_target_pairs={{8,0},{16,8},{24,16},{9,1},{17,9},{25,17},{10,2},{18,10},{26,18},{... | collective-permute-start | bytes 589832 | tf_op jit(solution)/shard_map/while/body/eval_jaxpr/ppermute | solution.py:16
  380.2 8.2 %copy-start.25 = (s32[128]{0:T(128)S(1)}, s32[128]{0:T(128)}, u32[]{:S(2)}) copy-start(s32[128]{0:T(128)} %copy-done.24) | copy-start | bytes 1540 | tf_op jit(solution)/shard_map/while
  388.5 8.8 %copy-start.24 = (s32[128]{0:T(128)}, s32[128]{0:T(128)S(1)}, u32[]{:S(2)}) copy-start(s32[128]{0:T(128)S(1)} %get-tuple-element.1288) | copy-start | bytes 1540 | tf_op jit(solution)/shard_map/while
  389.2 8.1 %copy-start.1 = (bf16[2,128,2304]{2,1,0:T(8,128)(2,1)S(1)}, bf16[2,128,2304]{2,1,0:T(8,128)(2,1)}, u32[]{:S(2)}) copy-start(bf16[2,128,2304]{2,1,0:T(8,128)(2,1)} %get-tuple-element.1285) | copy-start | bytes 3538948 | tf_op jit(solution)/shard_map/while
  392.5 12.7 %all-to-all-start.2 = ((bf16[8,16,768]{2,1,0:T(8,128)(2,1)}), bf16[8,16,768]{2,1,0:T(8,128)(2,1)S(1)}, u32[]{:S(2)}, u32[]{:S(2)}) async-start(bf16[8,16,768]{2,1,0:T(8,128)(2,1)} %bitcast.207), calls=%async_computation.2 | async-start | bytes 393216 | tf_op jit(solution)/shard_map/while/body/eval_jaxpr/all_to_all | solution.py:174
  412.3 21.0 %all-to-all-start.3 = ((bf16[8,16,2304]{2,1,0:T(8,128)(2,1)}), bf16[8,16,2304]{2,1,0:T(8,128)(2,1)S(1)}, u32[]{:S(2)}, u32[]{:S(2)}) async-start(bf16[8,16,2304]{2,1,0:T(8,128)(2,1)} %bitcast.209), calls=%async_computation.3 | async-start | bytes 1179648 | tf_op jit(solution)/shard_map/while/body/eval_jaxpr/all_to_all | solution.py:179
  439.0 9.5 %collective-permute-start.1 = (bf16[128,768]{1,0:T(8,128)(2,1)S(1)}, bf16[128,768]{1,0:T(8,128)(2,1)}, u32[]{:S(2)}, u32[]{:S(2)}) collective-permute-start(bf16[128,768]{1,0:T(8,128)(2,1)S(1)} %fusion.109), channel_id=1, source_target_pairs={{8,0},{16,8},{24,16},{9,1},{17,9},{25,17},{10,2},{18,10},{26,18},{... | collective-permute-start | bytes 589832 | tf_op jit(solution)/shard_map/while/body/eval_jaxpr/ppermute | solution.py:16
  440.3 8.2 %copy-start.25 = (s32[128]{0:T(128)S(1)}, s32[128]{0:T(128)}, u32[]{:S(2)}) copy-start(s32[128]{0:T(128)} %copy-done.24) | copy-start | bytes 1540 | tf_op jit(solution)/shard_map/while
  448.5 8.8 %copy-start.24 = (s32[128]{0:T(128)}, s32[128]{0:T(128)S(1)}, u32[]{:S(2)}) copy-start(s32[128]{0:T(128)S(1)} %get-tuple-element.1288) | copy-start | bytes 1540 | tf_op jit(solution)/shard_map/while
  449.2 8.1 %copy-start.1 = (bf16[2,128,2304]{2,1,0:T(8,128)(2,1)S(1)}, bf16[2,128,2304]{2,1,0:T(8,128)(2,1)}, u32[]{:S(2)}) copy-start(bf16[2,128,2304]{2,1,0:T(8,128)(2,1)} %get-tuple-element.1285) | copy-start | bytes 3538948 | tf_op jit(solution)/shard_map/while
  452.5 12.7 %all-to-all-start.2 = ((bf16[8,16,768]{2,1,0:T(8,128)(2,1)}), bf16[8,16,768]{2,1,0:T(8,128)(2,1)S(1)}, u32[]{:S(2)}, u32[]{:S(2)}) async-start(bf16[8,16,768]{2,1,0:T(8,128)(2,1)} %bitcast.207), calls=%async_computation.2 | async-start | bytes 393216 | tf_op jit(solution)/shard_map/while/body/eval_jaxpr/all_to_all | solution.py:174
  472.4 21.0 %all-to-all-start.3 = ((bf16[8,16,2304]{2,1,0:T(8,128)(2,1)}), bf16[8,16,2304]{2,1,0:T(8,128)(2,1)S(1)}, u32[]{:S(2)}, u32[]{:S(2)}) async-start(bf16[8,16,2304]{2,1,0:T(8,128)(2,1)} %bitcast.209), calls=%async_computation.3 | async-start | bytes 1179648 | tf_op jit(solution)/shard_map/while/body/eval_jaxpr/all_to_all | solution.py:179
  499.0 9.1 %collective-permute-start.1 = (bf16[128,768]{1,0:T(8,128)(2,1)S(1)}, bf16[128,768]{1,0:T(8,128)(2,1)}, u32[]{:S(2)}, u32[]{:S(2)}) collective-permute-start(bf16[128,768]{1,0:T(8,128)(2,1)S(1)} %fusion.109), channel_id=1, source_target_pairs={{8,0},{16,8},{24,16},{9,1},{17,9},{25,17},{10,2},{18,10},{26,18},{... | collective-permute-start | bytes 589832 | tf_op jit(solution)/shard_map/while/body/eval_jaxpr/ppermute | solution.py:16
  500.3 7.7 %copy-start.25 = (s32[128]{0:T(128)S(1)}, s32[128]{0:T(128)}, u32[]{:S(2)}) copy-start(s32[128]{0:T(128)} %copy-done.24) | copy-start | bytes 1540 | tf_op jit(solution)/shard_map/while
  508.1 8.8 %copy-start.24 = (s32[128]{0:T(128)}, s32[128]{0:T(128)S(1)}, u32[]{:S(2)}) copy-start(s32[128]{0:T(128)S(1)} %get-tuple-element.1288) | copy-start | bytes 1540 | tf_op jit(solution)/shard_map/while
  508.8 8.1 %copy-start.1 = (bf16[2,128,2304]{2,1,0:T(8,128)(2,1)S(1)}, bf16[2,128,2304]{2,1,0:T(8,128)(2,1)}, u32[]{:S(2)}) copy-start(bf16[2,128,2304]{2,1,0:T(8,128)(2,1)} %get-tuple-element.1285) | copy-start | bytes 3538948 | tf_op jit(solution)/shard_map/while
  512.1 12.7 %all-to-all-start.2 = ((bf16[8,16,768]{2,1,0:T(8,128)(2,1)}), bf16[8,16,768]{2,1,0:T(8,128)(2,1)S(1)}, u32[]{:S(2)}, u32[]{:S(2)}) async-start(bf16[8,16,768]{2,1,0:T(8,128)(2,1)} %bitcast.207), calls=%async_computation.2 | async-start | bytes 393216 | tf_op jit(solution)/shard_map/while/body/eval_jaxpr/all_to_all | solution.py:174
  531.9 21.0 %all-to-all-start.3 = ((bf16[8,16,2304]{2,1,0:T(8,128)(2,1)}), bf16[8,16,2304]{2,1,0:T(8,128)(2,1)S(1)}, u32[]{:S(2)}, u32[]{:S(2)}) async-start(bf16[8,16,2304]{2,1,0:T(8,128)(2,1)} %bitcast.209), calls=%async_computation.3 | async-start | bytes 1179648 | tf_op jit(solution)/shard_map/while/body/eval_jaxpr/all_to_all | solution.py:179
  558.6 9.1 %collective-permute-start.1 = (bf16[128,768]{1,0:T(8,128)(2,1)S(1)}, bf16[128,768]{1,0:T(8,128)(2,1)}, u32[]{:S(2)}, u32[]{:S(2)}) collective-permute-start(bf16[128,768]{1,0:T(8,128)(2,1)S(1)} %fusion.109), channel_id=1, source_target_pairs={{8,0},{16,8},{24,16},{9,1},{17,9},{25,17},{10,2},{18,10},{26,18},{... | collective-permute-start | bytes 589832 | tf_op jit(solution)/shard_map/while/body/eval_jaxpr/ppermute | solution.py:16
  559.9 7.7 %copy-start.25 = (s32[128]{0:T(128)S(1)}, s32[128]{0:T(128)}, u32[]{:S(2)}) copy-start(s32[128]{0:T(128)} %copy-done.24) | copy-start | bytes 1540 | tf_op jit(solution)/shard_map/while
  567.7 8.8 %copy-start.24 = (s32[128]{0:T(128)}, s32[128]{0:T(128)S(1)}, u32[]{:S(2)}) copy-start(s32[128]{0:T(128)S(1)} %get-tuple-element.1288) | copy-start | bytes 1540 | tf_op jit(solution)/shard_map/while
  568.4 8.1 %copy-start.1 = (bf16[2,128,2304]{2,1,0:T(8,128)(2,1)S(1)}, bf16[2,128,2304]{2,1,0:T(8,128)(2,1)}, u32[]{:S(2)}) copy-start(bf16[2,128,2304]{2,1,0:T(8,128)(2,1)} %get-tuple-element.1285) | copy-start | bytes 3538948 | tf_op jit(solution)/shard_map/while
  571.7 12.7 %all-to-all-start.2 = ((bf16[8,16,768]{2,1,0:T(8,128)(2,1)}), bf16[8,16,768]{2,1,0:T(8,128)(2,1)S(1)}, u32[]{:S(2)}, u32[]{:S(2)}) async-start(bf16[8,16,768]{2,1,0:T(8,128)(2,1)} %bitcast.207), calls=%async_computation.2 | async-start | bytes 393216 | tf_op jit(solution)/shard_map/while/body/eval_jaxpr/all_to_all | solution.py:174
  591.5 21.0 %all-to-all-start.3 = ((bf16[8,16,2304]{2,1,0:T(8,128)(2,1)}), bf16[8,16,2304]{2,1,0:T(8,128)(2,1)S(1)}, u32[]{:S(2)}, u32[]{:S(2)}) async-start(bf16[8,16,2304]{2,1,0:T(8,128)(2,1)} %bitcast.209), calls=%async_computation.3 | async-start | bytes 1179648 | tf_op jit(solution)/shard_map/while/body/eval_jaxpr/all_to_all | solution.py:179
  618.2 9.1 %collective-permute-start.1 = (bf16[128,768]{1,0:T(8,128)(2,1)S(1)}, bf16[128,768]{1,0:T(8,128)(2,1)}, u32[]{:S(2)}, u32[]{:S(2)}) collective-permute-start(bf16[128,768]{1,0:T(8,128)(2,1)S(1)} %fusion.109), channel_id=1, source_target_pairs={{8,0},{16,8},{24,16},{9,1},{17,9},{25,17},{10,2},{18,10},{26,18},{... | collective-permute-start | bytes 589832 | tf_op jit(solution)/shard_map/while/body/eval_jaxpr/ppermute | solution.py:16
  619.5 7.7 %copy-start.25 = (s32[128]{0:T(128)S(1)}, s32[128]{0:T(128)}, u32[]{:S(2)}) copy-start(s32[128]{0:T(128)} %copy-done.24) | copy-start | bytes 1540 | tf_op jit(solution)/shard_map/while
  627.3 117.8 %reduce-scatter.3.cloned.1.call-start = ((), (), s32[]{:S(2)}) async-start(), calls=%async_computation.6 | async-start | bytes 7962624 | tf_op jit(solution)/shard_map/reduce_scatter | solution.py:208
  (82 other events, 285.7 us)
Sparse Core Ops, SparseCore 0:
  627.4 37.8 reduce-scatter.4
  668.1 76.9 reduce-scatter.2
where the time goes:
time: 759 us; the launch traced here: 752 us
  waiting for transfers between devices  285 us (38%)
  starting transfers between devices  132 us (17%)
  local copies, waits for them, and re-layouts  115 us (15%)
  matrix products  113 us (15%)
  other arithmetic  74.4 us (10%)
  between operations  14.8 us (2%)
  blocking collectives  14.6 us (2%)
    reduce_scatter x1, waiting for transfers between devices, per_device(): lax.psum_scatter(qkv_total, 'tok', scatter_dimension=0, tiled=True)  79.9 us
    all_to_all x5, waiting for transfers between devices, forward_step(): lax.all_to_all(pack_home(projected), 'tok', split_axis=0, concat_axis=0,...  70.1 us
    all_to_all x5, waiting for transfers between devices, backward_step(): lax.all_to_all(pack_window(grad_window), 'tok', split_axis=0, concat_axis...  62.6 us
    dot_general x5, matrix products, backward_step(): jnp.einsum('td,tc->dc', kept_rows, grad_proj, preferred_element_type=jnp....  32.4 us
    all_to_all x5, starting transfers between devices, forward_step(): lax.all_to_all(pack_home(projected), 'tok', split_axis=0, concat_axis=0,...  32.2 us
    all_to_all x5, waiting for transfers between devices, forward_step(): lax.all_to_all(pack_window(mixed_window), 'tok', split_axis=0, concat_axi...  31.4 us
    ppermute x10, starting transfers between devices, from_behind(): lax.ppermute(value, axis, [(source, source + steps) for source in range(f...  27.8 us
    all_to_all x5, starting transfers between devices, backward_step(): lax.all_to_all(pack_window(grad_window), 'tok', split_axis=0, concat_axis...  25.6 us
  transfers between devices with their start and end apart: 32, of which 27 were waited for; matrix products, arithmetic and copies ran while one was open for 13% of the time, Pallas kernels for 0%

commit v1 on v0

--- a/solution.py
+++ b/solution.py
@@ -88,22 +88,22 @@
     out_matrix = out_weight[0]
     target_device = window_slot // row_count
     send_order = jnp.argsort(target_device, stable=True)
-    home_place = jnp.argsort(send_order)
     back_order = jnp.argsort(slot_token)
     slot_place = jnp.argsort(back_order)
 
     def pack_home(rows_in):
         return jnp.take(rows_in, send_order, axis=0)
 
-    def place_home(rows_in):
-        return jnp.take(rows_in, home_place, axis=0)
-
-    def pack_window(rows_in):
-        return jnp.take(rows_in, back_order, axis=0)
-
     def place_window(rows_in):
         return jnp.take(rows_in, slot_place, axis=0)
 
+    both = jnp.concatenate([tokens, cotangent], axis=0).transpose(1, 0, 2)
+    both = both.reshape(row_count, -1)
+    both = place_window(
+        lax.all_to_all(pack_home(both), "tok", split_axis=0, concat_axis=0, tiled=True)
+    )
+    both = both.reshape(row_count, 2 * micro_count, feature_width).transpose(1, 0, 2)
+    tokens, cotangent = both[:micro_count], both[micro_count:]
     steps_total = micro_count + section_count - 1
     zero_rows = jnp.zeros((micro_count, row_count, feature_width), jnp.bfloat16)
     start_carry = (
@@ -127,15 +127,8 @@
         projected = jnp.dot(normed, qkv_matrix, preferred_element_type=jnp.float32).astype(
             jnp.bfloat16
         )
-        window_rows = place_window(
-            lax.all_to_all(pack_home(projected), "tok", split_axis=0, concat_axis=0, tiled=True)
-        )
-        mixed_window = window_forward(window_rows)
-        mixed_rows = place_home(
-            lax.all_to_all(
-                pack_window(mixed_window), "tok", split_axis=0, concat_axis=0, tiled=True
-            )
-        )
+        window_rows = projected
+        mixed_rows = window_forward(window_rows)
         layer_out = (
             layer_in.astype(jnp.float32)
             + jnp.dot(mixed_rows, out_matrix, preferred_element_type=jnp.float32)
@@ -171,13 +164,7 @@
         grad_mixed = jnp.einsum(
             "te,de->td", grad_layer, out_matrix, preferred_element_type=jnp.float32
         ).astype(jnp.bfloat16)
-        grad_arrived = lax.all_to_all(
-            pack_home(grad_mixed), "tok", split_axis=0, concat_axis=0, tiled=True
-        )
-        grad_window = window_backward(window_rows, place_window(grad_arrived))
-        grad_proj = place_home(
-            lax.all_to_all(pack_window(grad_window), "tok", split_axis=0, concat_axis=0, tiled=True)
-        )
+        grad_proj = window_backward(window_rows, grad_mixed)
         qkv_total = qkv_total + weight_on * jnp.einsum(
             "td,tc->dc", kept_rows, grad_proj, preferred_element_type=jnp.float32
         )

time: 759 us -> 567 us (0.75)
  waiting for transfers between devices: 285 us -> 119 us
  starting transfers between devices: 132 us -> 29 us
  local copies, waits for them, and re-layouts: 115 us -> 176 us
  matrix products: 113 us -> 151 us
  other arithmetic: 74.4 us -> 50.2 us
    all_to_all x20 -> x1, waiting for transfers between devices: 164 us -> 15 us  [per_device(): lax.all_to_all(pack_home(both), 'tok', split_axis=0, concat_axis=0, tiled...]
    all_to_all x20 -> x1, starting transfers between devices: 104 us -> 6.38 us  [per_device(): lax.all_to_all(pack_home(both), 'tok', split_axis=0, concat_axis=0, tiled...]
    convert_element_type x10 -> x15, local copies, waits for them, and re-layouts: 7.7 us -> 30.4 us  [window_forward(): return mixed_rows.reshape(window_rows.shape[0], -1).astype(jnp.bfloat16)]
    ppermute x10, waiting for transfers between devices: 19.2 us -> 0.03 us  [from_behind(): lax.ppermute(value, axis, [(source, source + steps) for source in range(f...]
    gather x20 -> x0, local copies, waits for them, and re-layouts: 19 us -> none  [the longest x10 9.8 us: pack_window(): return jnp.take(rows_in, back_order, axis=0)]
    convert_element_type x5 -> x10, local copies, waits for them, and re-layouts: 4.59 us -> 22.7 us  [window_backward(): return stacked.reshape(row_total, -1).astype(jnp.bfloat16)]
    slice x10, local copies, waits for them, and re-layouts: 11.3 us -> 25.5 us  [window_split(): return (shaped[:, :, 0], shaped[:, :, 1], shaped[:, :, 2], head_dim)]
    while x220 -> x170, local copies, waits for them, and re-layouts: 7.73 us -> 21.1 us
  transfers between devices with their start and end apart: 32 -> 13, of which waited for: 27 -> 3; matrix products, arithmetic and copies ran while one was open for 13% -> 13% of each run, Pallas kernels for 0% -> 0%
where the time goes in v1:
time: 567 us; the launch traced here: 560 us
  local copies, waits for them, and re-layouts  176 us (31%)
  matrix products  151 us (27%)
  waiting for transfers between devices  119 us (21%)
  other arithmetic  50.2 us (9%)
  starting transfers between devices  29 us (5%)
  blocking collectives  17.6 us (3%)
  between operations  14.8 us (3%)
    reduce_scatter x1, waiting for transfers between devices, per_device(): lax.psum_scatter(qkv_total, 'tok', scatter_dimension=0, tiled=True)  79.5 us
    dot_general x5, matrix products, backward_step(): jnp.einsum('td,tc->dc', kept_rows, grad_proj, preferred_element_type=jnp....  35.2 us
    convert_element_type x15, local copies, waits for them, and re-layouts, window_forward(): return mixed_rows.reshape(window_rows.shape[0], -1).astype(jnp.bfloat16)  30.4 us
    reshape x10, local copies, waits for them, and re-layouts, window_split(): window_rows.reshape(row_total // WINDOW, WINDOW, 3, HEADS, head_dim)  28.4 us
    sub x10, matrix products, window_soft(): return jax.nn.softmax(scores, axis=-1)  26.8 us
    slice x10, local copies, waits for them, and re-layouts, window_split(): return (shaped[:, :, 0], shaped[:, :, 1], shaped[:, :, 2], head_dim)  25.5 us
    reduce_scatter x1, waiting for transfers between devices, per_device(): lax.psum_scatter(out_total, 'tok', scatter_dimension=0, tiled=True)  24 us
    convert_element_type x10, local copies, waits for them, and re-layouts, window_backward(): return stacked.reshape(row_total, -1).astype(jnp.bfloat16)  22.7 us
  transfers between devices with their start and end apart: 13, of which 3 were waited for; matrix products, arithmetic and copies ran while one was open for 13% of the time, Pallas kernels for 0%

profile of v1, /device:TPU:1, one launch (start us, length us, event | category | flops | bytes accessed | tf_op | source)
XLA Modules:
  0.0 559.7 jit_solution(5081808074158784219)
XLA Ops:
  7.8 2.5 sort.48
  13.7 6.4 %all-to-all-start = ((bf16[8,16,3072]{2,1,0:T(8,128)(2,1)}), bf16[8,16,3072]{2,1,0:T(8,128)(2,1)S(1)}, u32[]{:S(2)}, u32[]{:S(2)}) async-start(bf16[8,16,3072]{2,1,0:T(8,128)(2,1)} %bitcast.12), calls=%async_computation | async-start | bytes 1572864 | tf_op jit(solution)/shard_map/all_to_all | solution.py:103
  20.2 2.5 sort.49
  22.7 2.5 sort.50
  25.3 15.0 %all-to-all-done = bf16[8,16,3072]{2,1,0:T(8,128)(2,1)S(1)} async-done(((bf16[8,16,3072]{2,1,0:T(8,128)(2,1)}), bf16[8,16,3072]{2,1,0:T(8,128)(2,1)S(1)}, u32[]{:S(2)}, u32[]{:S(2)}) %all-to-all-start) | async-done | bytes 786464 | tf_op jit(solution)/shard_map/all_to_all | solution.py:103
  46.6 176.9 %while.44 = (s32[]{:T(128)}, bf16[128,768]{1,0:T(8,128)(2,1)}, bf16[2,128,768]{2,1,0:T(8,128)(2,1)}, bf16[2,128,768]{2,1,0:T(8,128)(2,1)}, bf16[2,128,768]{2,1,0...) while((s32[]{:T(128)}, bf16[128,768]{1,0:T(8,128)(2,1)}, ...), condition=%wide.region_7.9_spmd, body=%wide.region_3.8_spmd.sunk | while | flops 625657536 | bytes 19886976 | solution.py:143
  51.9 2.9 bitcast_dynamic-update-slice_fusion.7
  54.8 2.8 reshape.165
  64.5 2.8 fusion.88
  73.7 3.9 collective-permute-start
  88.0 2.9 bitcast_dynamic-update-slice_fusion.7
  90.9 2.8 reshape.165
  100.6 2.8 fusion.88
  109.8 3.1 collective-permute-start
  123.4 2.9 bitcast_dynamic-update-slice_fusion.7
  126.2 2.8 reshape.165
  135.9 2.8 fusion.88
  145.1 3.8 collective-permute-start
  159.2 2.9 bitcast_dynamic-update-slice_fusion.7
  162.1 2.8 reshape.165
  171.8 2.8 fusion.88
  181.0 2.8 collective-permute-start
  194.1 2.9 bitcast_dynamic-update-slice_fusion.7
  197.0 2.8 reshape.165
  206.7 2.8 fusion.88
  215.9 2.6 collective-permute-start
  224.2 205.0 %while.45 = (s32[]{:T(128)}, bf16[128,768]{1,0:T(8,128)(2,1)}, f32[768,2304]{1,0:T(8,128)}, f32[768,768]{1,0:T(8,128)}, f32[768]{0:T(1024)S(1)}, /*index=5*/pred...) while((s32[]{:T(128)}, bf16[128,768]{1,0:T(8,128)(2,1)}, ...), condition=%wide.region_15.17_spmd.clone, body=%wide.region_8.16_spmd.clone.sunk | while | flops 1250132352 | bytes 67434728 | solution.py:191
  226.1 2.8 reshape.167
  228.9 2.6 fusion.103
  237.8 3.1 fusion.104
  246.4 2.9 convert_element_type.236
  250.9 2.6 fusion.107
  255.8 5.3 select_add_fusion.6
  265.4 2.8 reshape.167
  268.2 2.6 fusion.103
  272.6 2.5 convolution_convert_fusion.4
  277.1 3.1 fusion.104
  285.7 2.9 convert_element_type.236
  290.2 2.6 fusion.107
  295.1 7.5 %select_add_fusion.6 = f32[768,2304]{1,0:T(8,128)} fusion(f32[768,2304]{1,0:T(8,128)} %get-tuple-element.977, bf16[128,2304]{1,0:T(8,128)(2,1)} %convert_element_type.236, f32[]{:T(128)S(6)} %convert_element_type.237, pred[]{:T(512)S(6)} %compare.17, bf16[2,128,768]{2,1,0:T(8,128)(2,1)} %get-tuple-element.1007, s32[]{:T(128)S(6)} %min.45), kind=kOutput, calls=%fused_computation.36.clone.1 | convolution fusion | flops 458293248 | bytes 14942217 | tf_op jit(solution)/shard_map/while/body/eval_jaxpr/td,tc->dc/dot_general | solution.py:168
  306.8 2.8 reshape.167
  309.7 2.6 fusion.103
  314.0 2.5 convolution_convert_fusion.4
  318.6 3.1 fusion.104
  327.1 2.9 convert_element_type.236
  331.7 2.6 fusion.107
  336.5 7.5 %select_add_fusion.6 = f32[768,2304]{1,0:T(8,128)} fusion(f32[768,2304]{1,0:T(8,128)} %get-tuple-element.977, bf16[128,2304]{1,0:T(8,128)(2,1)} %convert_element_type.236, f32[]{:T(128)S(6)} %convert_element_type.237, pred[]{:T(512)S(6)} %compare.17, bf16[2,128,768]{2,1,0:T(8,128)(2,1)} %get-tuple-element.1007, s32[]{:T(128)S(6)} %min.45), kind=kOutput, calls=%fused_computation.36.clone.1 | convolution fusion | flops 458293248 | bytes 14942217 | tf_op jit(solution)/shard_map/while/body/eval_jaxpr/td,tc->dc/dot_general | solution.py:168
  348.2 2.8 reshape.167
  351.1 2.6 fusion.103
  355.4 2.5 convolution_convert_fusion.4
  360.0 3.1 fusion.104
  368.6 2.9 convert_element_type.236
  373.1 2.6 fusion.107
  377.9 7.5 %select_add_fusion.6 = f32[768,2304]{1,0:T(8,128)} fusion(f32[768,2304]{1,0:T(8,128)} %get-tuple-element.977, bf16[128,2304]{1,0:T(8,128)(2,1)} %convert_element_type.236, f32[]{:T(128)S(6)} %convert_element_type.237, pred[]{:T(512)S(6)} %compare.17, bf16[2,128,768]{2,1,0:T(8,128)(2,1)} %get-tuple-element.1007, s32[]{:T(128)S(6)} %min.45), kind=kOutput, calls=%fused_computation.36.clone.1 | convolution fusion | flops 458293248 | bytes 14942217 | tf_op jit(solution)/shard_map/while/body/eval_jaxpr/td,tc->dc/dot_general | solution.py:168
  389.7 2.8 reshape.167
  392.5 2.6 fusion.103
  396.9 2.5 convolution_convert_fusion.4
  401.4 3.1 fusion.104
  410.0 2.9 convert_element_type.236
  414.5 2.6 fusion.107
  419.4 7.5 %select_add_fusion.6 = f32[768,2304]{1,0:T(8,128)} fusion(f32[768,2304]{1,0:T(8,128)} %get-tuple-element.977, bf16[128,2304]{1,0:T(8,128)(2,1)} %convert_element_type.236, f32[]{:T(128)S(6)} %convert_element_type.237, pred[]{:T(512)S(6)} %compare.17, bf16[2,128,768]{2,1,0:T(8,128)(2,1)} %get-tuple-element.1007, s32[]{:T(128)S(6)} %min.45), kind=kOutput, calls=%fused_computation.36.clone.1 | convolution fusion | flops 458293248 | bytes 14942217 | tf_op jit(solution)/shard_map/while/body/eval_jaxpr/td,tc->dc/dot_general | solution.py:168
  431.2 17.6 %all-reduce = f32[768]{0:T(1024)S(1)} all-reduce(f32[768]{0:T(1024)S(1)} %get-tuple-element.576), channel_id=4, replica_groups=mesh['section'=4,'tok'=8] {'tok'}, use_global_device_ids=true, to_apply=%region_18.20.clone | all-reduce | flops 768 | bytes 6144
  449.4 24.0 %reduce-scatter.5.cloned.1.call-done = f32[96,768]{1,0:T(8,128)} async-done(((f32[768,768]{1,0:T(8,128)}), f32[96,768]{1,0:T(8,128)}) %reduce-scatter.5.cloned.1.call-update) | async-done | bytes 294928 | tf_op jit(solution)/shard_map/reduce_scatter | solution.py:196
  473.4 79.5 %reduce-scatter.3.cloned.1.call-done = f32[96,2304]{1,0:T(8,128)} async-done(((f32[768,2304]{1,0:T(8,128)}), f32[96,2304]{1,0:T(8,128)}) %reduce-scatter.3.cloned.1.call-update) | async-done | bytes 884752 | tf_op jit(solution)/shard_map/reduce_scatter | solution.py:195
  (387 shorter events, 219.5 us)
Async XLA Ops:
  12.7 7.4 %copy-start.19 = (s32[128]{0:T(128)S(1)}, s32[128]{0:T(128)}, u32[]{:S(2)}) copy-start(s32[128]{0:T(128)} %param.16) | copy-start | bytes 1540
  13.7 26.5 %all-to-all-start = ((bf16[8,16,3072]{2,1,0:T(8,128)(2,1)}), bf16[8,16,3072]{2,1,0:T(8,128)(2,1)S(1)}, u32[]{:S(2)}, u32[]{:S(2)}) async-start(bf16[8,16,3072]{2,1,0:T(8,128)(2,1)} %bitcast.12), calls=%async_computation | async-start | bytes 1572864 | tf_op jit(solution)/shard_map/all_to_all | solution.py:103
  20.1 453.3 %reduce-scatter.5.cloned.1.call-start = ((), (), s32[]{:S(2)}) async-start(), calls=%async_computation.4 | async-start | bytes 2654208 | tf_op jit(solution)/shard_map/reduce_scatter | solution.py:196
  41.5 5.1 copy-start
  41.5 5.1 copy-start.16
  73.7 8.9 %collective-permute-start = (bf16[128,768]{1,0:T(8,128)(2,1)}, bf16[128,768]{1,0:T(8,128)(2,1)}, u32[]{:S(2)}, u32[]{:S(2)}) collective-permute-start(bf16[128,768]{1,0:T(8,128)(2,1)} %fusion.89), channel_id=1, source_target_pairs={{0,8},{8,16},{16,24},{1,9},{9,17},{17,25},{2,10},{10,18},{18,26},{... | collective-permute-start | bytes 589832 | tf_op jit(solution)/shard_map/while/body/eval_jaxpr/ppermute | solution.py:16
  109.8 8.2 %collective-permute-start = (bf16[128,768]{1,0:T(8,128)(2,1)}, bf16[128,768]{1,0:T(8,128)(2,1)}, u32[]{:S(2)}, u32[]{:S(2)}) collective-permute-start(bf16[128,768]{1,0:T(8,128)(2,1)} %fusion.89), channel_id=1, source_target_pairs={{0,8},{8,16},{16,24},{1,9},{9,17},{17,25},{2,10},{10,18},{18,26},{... | collective-permute-start | bytes 589832 | tf_op jit(solution)/shard_map/while/body/eval_jaxpr/ppermute | solution.py:16
  145.1 8.7 %collective-permute-start = (bf16[128,768]{1,0:T(8,128)(2,1)}, bf16[128,768]{1,0:T(8,128)(2,1)}, u32[]{:S(2)}, u32[]{:S(2)}) collective-permute-start(bf16[128,768]{1,0:T(8,128)(2,1)} %fusion.89), channel_id=1, source_target_pairs={{0,8},{8,16},{16,24},{1,9},{9,17},{17,25},{2,10},{10,18},{18,26},{... | collective-permute-start | bytes 589832 | tf_op jit(solution)/shard_map/while/body/eval_jaxpr/ppermute | solution.py:16
  181.0 7.8 %collective-permute-start = (bf16[128,768]{1,0:T(8,128)(2,1)}, bf16[128,768]{1,0:T(8,128)(2,1)}, u32[]{:S(2)}, u32[]{:S(2)}) collective-permute-start(bf16[128,768]{1,0:T(8,128)(2,1)} %fusion.89), channel_id=1, source_target_pairs={{0,8},{8,16},{16,24},{1,9},{9,17},{17,25},{2,10},{10,18},{18,26},{... | collective-permute-start | bytes 589832 | tf_op jit(solution)/shard_map/while/body/eval_jaxpr/ppermute | solution.py:16
  215.9 7.6 %collective-permute-start = (bf16[128,768]{1,0:T(8,128)(2,1)}, bf16[128,768]{1,0:T(8,128)(2,1)}, u32[]{:S(2)}, u32[]{:S(2)}) collective-permute-start(bf16[128,768]{1,0:T(8,128)(2,1)} %fusion.89), channel_id=1, source_target_pairs={{0,8},{8,16},{16,24},{1,9},{9,17},{17,25},{2,10},{10,18},{18,26},{... | collective-permute-start | bytes 589832 | tf_op jit(solution)/shard_map/while/body/eval_jaxpr/ppermute | solution.py:16
  241.0 1.9 copy-start.12
  241.0 1.9 copy-start.15
  241.0 2.2 copy-start.9
  250.9 2.6 copy-start.5
  250.9 2.6 copy-start.7
  250.9 2.6 copy-start.17
  250.9 2.6 copy-start.18
  254.4 7.6 %collective-permute-start.1 = (bf16[128,768]{1,0:T(8,128)(2,1)}, bf16[128,768]{1,0:T(8,128)(2,1)}, u32[]{:S(2)}, u32[]{:S(2)}) collective-permute-start(bf16[128,768]{1,0:T(8,128)(2,1)} %fusion.108), channel_id=1, source_target_pairs={{8,0},{16,8},{24,16},{9,1},{17,9},{25,17},{10,2},{18,10},{26,18},{... | collective-permute-start | bytes 589832 | tf_op jit(solution)/shard_map/while/body/eval_jaxpr/ppermute | solution.py:16
  255.7 5.4 copy-start.2
  255.8 5.4 copy-start.6
  255.8 5.4 copy-start.13
  280.3 1.9 copy-start.12
  280.3 1.9 copy-start.15
  280.3 2.2 copy-start.9
  290.2 2.6 copy-start.5
  290.2 2.6 copy-start.7
  290.2 2.6 copy-start.17
  290.2 2.6 copy-start.18
  293.7 9.7 %collective-permute-start.1 = (bf16[128,768]{1,0:T(8,128)(2,1)}, bf16[128,768]{1,0:T(8,128)(2,1)}, u32[]{:S(2)}, u32[]{:S(2)}) collective-permute-start(bf16[128,768]{1,0:T(8,128)(2,1)} %fusion.108), channel_id=1, source_target_pairs={{8,0},{16,8},{24,16},{9,1},{17,9},{25,17},{10,2},{18,10},{26,18},{... | collective-permute-start | bytes 589832 | tf_op jit(solution)/shard_map/while/body/eval_jaxpr/ppermute | solution.py:16
  295.0 7.5 %copy-start.2 = (f32[768,768]{1,0:T(8,128)S(1)}, f32[768,768]{1,0:T(8,128)}, u32[]{:S(2)}) copy-start(f32[768,768]{1,0:T(8,128)} %get-tuple-element.978) | copy-start | bytes 7077892 | tf_op jit(solution)/shard_map/while
  295.1 7.5 %copy-start.6 = (bf16[128,768]{1,0:T(8,128)(2,1)S(1)}, bf16[128,768]{1,0:T(8,128)(2,1)}, u32[]{:S(2)}) copy-start(bf16[128,768]{1,0:T(8,128)(2,1)} %copy-done.4) | copy-start | bytes 589828 | tf_op jit(solution)/shard_map/while
  295.1 7.5 %copy-start.13 = (bf16[2,128,768]{2,1,0:T(8,128)(2,1)S(1)}, bf16[2,128,768]{2,1,0:T(8,128)(2,1)}, u32[]{:S(2)}) copy-start(bf16[2,128,768]{2,1,0:T(8,128)(2,1)} %get-tuple-element.1008) | copy-start | bytes 1179652 | tf_op jit(solution)/shard_map/while
  321.7 1.9 copy-start.12
  321.7 1.9 copy-start.15
  321.7 2.2 copy-start.9
  331.6 2.6 copy-start.5
  331.6 2.6 copy-start.7
  331.6 2.6 copy-start.17
  331.6 2.6 copy-start.18
  335.2 9.7 %collective-permute-start.1 = (bf16[128,768]{1,0:T(8,128)(2,1)}, bf16[128,768]{1,0:T(8,128)(2,1)}, u32[]{:S(2)}, u32[]{:S(2)}) collective-permute-start(bf16[128,768]{1,0:T(8,128)(2,1)} %fusion.108), channel_id=1, source_target_pairs={{8,0},{16,8},{24,16},{9,1},{17,9},{25,17},{10,2},{18,10},{26,18},{... | collective-permute-start | bytes 589832 | tf_op jit(solution)/shard_map/while/body/eval_jaxpr/ppermute | solution.py:16
  336.5 7.5 %copy-start.2 = (f32[768,768]{1,0:T(8,128)S(1)}, f32[768,768]{1,0:T(8,128)}, u32[]{:S(2)}) copy-start(f32[768,768]{1,0:T(8,128)} %get-tuple-element.978) | copy-start | bytes 7077892 | tf_op jit(solution)/shard_map/while
  336.5 7.5 %copy-start.6 = (bf16[128,768]{1,0:T(8,128)(2,1)S(1)}, bf16[128,768]{1,0:T(8,128)(2,1)}, u32[]{:S(2)}) copy-start(bf16[128,768]{1,0:T(8,128)(2,1)} %copy-done.4) | copy-start | bytes 589828 | tf_op jit(solution)/shard_map/while
  336.5 7.5 %copy-start.13 = (bf16[2,128,768]{2,1,0:T(8,128)(2,1)S(1)}, bf16[2,128,768]{2,1,0:T(8,128)(2,1)}, u32[]{:S(2)}) copy-start(bf16[2,128,768]{2,1,0:T(8,128)(2,1)} %get-tuple-element.1008) | copy-start | bytes 1179652 | tf_op jit(solution)/shard_map/while
  363.1 1.9 copy-start.15
  363.1 2.2 copy-start.9
  373.0 2.6 copy-start.5
  373.0 2.6 copy-start.7
  373.1 2.6 copy-start.17
  373.1 2.6 copy-start.18
  376.6 9.7 %collective-permute-start.1 = (bf16[128,768]{1,0:T(8,128)(2,1)}, bf16[128,768]{1,0:T(8,128)(2,1)}, u32[]{:S(2)}, u32[]{:S(2)}) collective-permute-start(bf16[128,768]{1,0:T(8,128)(2,1)} %fusion.108), channel_id=1, source_target_pairs={{8,0},{16,8},{24,16},{9,1},{17,9},{25,17},{10,2},{18,10},{26,18},{... | collective-permute-start | bytes 589832 | tf_op jit(solution)/shard_map/while/body/eval_jaxpr/ppermute | solution.py:16
  377.9 7.5 %copy-start.2 = (f32[768,768]{1,0:T(8,128)S(1)}, f32[768,768]{1,0:T(8,128)}, u32[]{:S(2)}) copy-start(f32[768,768]{1,0:T(8,128)} %get-tuple-element.978) | copy-start | bytes 7077892 | tf_op jit(solution)/shard_map/while
  377.9 7.5 %copy-start.6 = (bf16[128,768]{1,0:T(8,128)(2,1)S(1)}, bf16[128,768]{1,0:T(8,128)(2,1)}, u32[]{:S(2)}) copy-start(bf16[128,768]{1,0:T(8,128)(2,1)} %copy-done.4) | copy-start | bytes 589828 | tf_op jit(solution)/shard_map/while
  377.9 7.5 %copy-start.13 = (bf16[2,128,768]{2,1,0:T(8,128)(2,1)S(1)}, bf16[2,128,768]{2,1,0:T(8,128)(2,1)}, u32[]{:S(2)}) copy-start(bf16[2,128,768]{2,1,0:T(8,128)(2,1)} %get-tuple-element.1008) | copy-start | bytes 1179652 | tf_op jit(solution)/shard_map/while
  404.5 1.9 copy-start.15
  404.5 2.2 copy-start.9
  414.5 2.6 copy-start.5
  414.5 2.6 copy-start.7
  414.5 2.6 copy-start.17
  414.5 2.6 copy-start.18
  418.0 9.7 %collective-permute-start.1 = (bf16[128,768]{1,0:T(8,128)(2,1)}, bf16[128,768]{1,0:T(8,128)(2,1)}, u32[]{:S(2)}, u32[]{:S(2)}) collective-permute-start(bf16[128,768]{1,0:T(8,128)(2,1)} %fusion.108), channel_id=1, source_target_pairs={{8,0},{16,8},{24,16},{9,1},{17,9},{25,17},{10,2},{18,10},{26,18},{... | collective-permute-start | bytes 589832 | tf_op jit(solution)/shard_map/while/body/eval_jaxpr/ppermute | solution.py:16
  419.3 7.5 %copy-start.2 = (f32[768,768]{1,0:T(8,128)S(1)}, f32[768,768]{1,0:T(8,128)}, u32[]{:S(2)}) copy-start(f32[768,768]{1,0:T(8,128)} %get-tuple-element.978) | copy-start | bytes 7077892 | tf_op jit(solution)/shard_map/while
  419.3 7.5 %copy-start.6 = (bf16[128,768]{1,0:T(8,128)(2,1)S(1)}, bf16[128,768]{1,0:T(8,128)(2,1)}, u32[]{:S(2)}) copy-start(bf16[128,768]{1,0:T(8,128)(2,1)} %copy-done.4) | copy-start | bytes 589828 | tf_op jit(solution)/shard_map/while
  419.3 7.5 %copy-start.13 = (bf16[2,128,768]{2,1,0:T(8,128)(2,1)S(1)}, bf16[2,128,768]{2,1,0:T(8,128)(2,1)}, u32[]{:S(2)}) copy-start(bf16[2,128,768]{2,1,0:T(8,128)(2,1)} %get-tuple-element.1008) | copy-start | bytes 1179652 | tf_op jit(solution)/shard_map/while
  429.2 123.7 %reduce-scatter.3.cloned.1.call-start = ((), (), s32[]{:S(2)}) async-start(), calls=%async_computation.3 | async-start | bytes 7962624 | tf_op jit(solution)/shard_map/reduce_scatter | solution.py:195
  (38 other events, 39.1 us)
Sparse Core Ops, SparseCore 0:
  429.3 44.0 reduce-scatter.4
  476.3 76.5 reduce-scatter.2

commit v2 on v1

v2 whole, which is shorter than its diff:
```python
import functools

import jax
import jax.numpy as jnp
from jax import lax
from jax.experimental import pallas as pl
from jax.experimental.pallas import tpu as pltpu
from jax.sharding import PartitionSpec as P

HEADS = 12
WINDOW = 32
PAIR = 128
EPSILON = 1e-06
F32 = jnp.float32
BF16 = jnp.bfloat16


def dot_nn(a, b):
    return lax.dot_general(a, b, (((1,), (0,)), ((), ())), preferred_element_type=F32)


def dot_nt(a, b):
    return lax.dot_general(a, b, (((1,), (1,)), ((), ())), preferred_element_type=F32)


def dot_tn(a, b):
    return lax.dot_general(a, b, (((0,), (0,)), ((), ())), preferred_element_type=F32)


def to_section(src, dst, send, recv, section):
    return pltpu.make_async_remote_copy(
        src_ref=src,
        dst_ref=dst,
        send_sem=send,
        recv_sem=recv,
        device_id={"section": section},
        device_id_type=pl.DeviceIdType.MESH,
    )


def chain_kernel(
    sections, micros, enter_ref, gain_ref, wqkv_ref, wout_ref,
    dqkv_ref, dout_ref, dgain_ref,
    x_keep, g_keep, n_keep, a_keep, qkv_keep, p_keep, dp_keep, xbox, gbox,
    fwd_send, fwd_recv, bwd_send, bwd_recv,
):
    rows, width = enter_ref.shape[1], enter_ref.shape[2]
    head_dim = width // HEADS
    temper = head_dim ** (-0.5)
    here = lax.axis_index("section")
    first, last = here == 0, here == sections - 1
    barrier = pltpu.get_barrier_semaphore()

    @pl.when(jnp.logical_not(first))
    def _():
        pl.semaphore_signal(barrier, inc=1, device_id={"section": here - 1},
                            device_id_type=pl.DeviceIdType.MESH)

    @pl.when(jnp.logical_not(last))
    def _():
        pl.semaphore_signal(barrier, inc=1, device_id={"section": here + 1},
                            device_id_type=pl.DeviceIdType.MESH)

    middle = jnp.logical_not(jnp.logical_or(first, last))

    @pl.when(middle)
    def _():
        pl.semaphore_wait(barrier, 2)

    @pl.when(jnp.logical_not(middle))
    def _():
        pl.semaphore_wait(barrier, 1)

    gain = gain_ref[...]
    lane = lax.broadcasted_iota(jnp.int32, (1, PAIR), 1)
    low = jnp.where(lane < head_dim, 1.0, 0.0).astype(BF16)
    high = jnp.where(lane < head_dim, 0.0, 1.0).astype(BF16)
    row_window = lax.broadcasted_iota(jnp.int32, (rows, rows), 0) // WINDOW
    col_window = lax.broadcasted_iota(jnp.int32, (rows, rows), 1) // WINDOW
    hide = jnp.where(row_window == col_window, 0.0, -1e30)
    hide = jnp.concatenate([hide, hide], axis=0)

    def two(value):
        return jnp.concatenate([value * low, value * high], axis=0)

    def beside(value):
        return jnp.concatenate([value[:rows], value[rows:]], axis=1)

    def fwd_copy(m):
        return to_section(xbox.at[m], x_keep.at[m], fwd_send.at[m], fwd_recv.at[m], here + 1)

    def bwd_copy(m):
        return to_section(gbox.at[m], g_keep.at[m], bwd_send.at[m], bwd_recv.at[m], here - 1)

    def factor_of(x):
        return lax.rsqrt(jnp.mean(x * x, axis=-1, keepdims=True) + EPSILON)

    for m in range(micros):
        span = slice(m * rows, (m + 1) * rows)

        @pl.when(first)
        def _():
            x_keep[m] = enter_ref[m]

        @pl.when(jnp.logical_not(first))
        def _():
            fwd_copy(m).wait_recv()

        x = x_keep[m].astype(F32)
        normed = (x * factor_of(x) * gain).astype(BF16)
        n_keep[span, :] = normed
        for c in range(0, 3 * width, 256):
            qkv_keep[m, :, c:c + 256] = dot_nn(normed, wqkv_ref[:, c:c + 256]).astype(BF16)
        for j in range(width // PAIR):
            c = j * PAIR
            q = qkv_keep[m, :, c:c + PAIR]
            k = qkv_keep[m, :, width + c:width + c + PAIR]
            v = qkv_keep[m, :, 2 * width + c:2 * width + c + PAIR]
            scores = dot_nt(two(q), k) * temper + hide
            top = jnp.max(scores, axis=-1, keepdims=True)
            raised = jnp.exp(scores - top)
            soft = raised / jnp.sum(raised, axis=-1, keepdims=True)
            p_keep[m, j] = soft
            mixed = dot_nn(beside(soft.astype(BF16)), two(v))
            a_keep[span, c:c + PAIR] = mixed.astype(BF16)

        @pl.when(jnp.logical_not(last))
        def _():
            xbox[m] = (x_keep[m].astype(F32) + dot_nn(a_keep[span, :], wout_ref[...])).astype(BF16)
            fwd_copy(m).start()

    for m in range(micros):
        span = slice(m * rows, (m + 1) * rows)

        @pl.when(last)
        def _():
            g_keep[m] = enter_ref[micros + m]

        @pl.when(jnp.logical_not(last))
        def _():
            bwd_copy(m).wait_recv()

        grad_mixed = dot_nt(g_keep[m], wout_ref[...]).astype(BF16)
        for j in range(width // PAIR):
            c = j * PAIR
            q = qkv_keep[m, :, c:c + PAIR]
            k = qkv_keep[m, :, width + c:width + c + PAIR]
            v = qkv_keep[m, :, 2 * width + c:2 * width + c + PAIR]
            dw = two(grad_mixed[:, c:c + PAIR])
            soft = p_keep[m, j]
            grad_soft = dot_nt(dw, v)
            grad_scores = soft * (grad_soft - jnp.sum(soft * grad_soft, axis=-1, keepdims=True))
            low_scores = grad_scores.astype(BF16)
            dq = dot_nn(beside(low_scores), two(k)) * temper
            dk = dot_tn(low_scores, two(q)) * temper
            dv = dot_tn(soft.astype(BF16), dw)
            dp_keep[span, c:c + PAIR] = dq.astype(BF16)
            dp_keep[span, width + c:width + c + PAIR] = dk.astype(BF16)
            dp_keep[span, 2 * width + c:2 * width + c + PAIR] = dv.astype(BF16)
        grad_normed = dot_nt(dp_keep[span, :], wqkv_ref[...])
        x = x_keep[m].astype(F32)
        factor = factor_of(x)

        @pl.when(jnp.logical_not(first))
        def _():
            scaled = gain * grad_normed
            inner = jnp.mean(scaled * x, axis=-1, keepdims=True)
            gbox[m] = (g_keep[m].astype(F32) + factor * scaled - x * (factor * factor * factor) * inner).astype(BF16)
            bwd_copy(m).start()

        piece = jnp.sum(grad_normed * x * factor, axis=0, keepdims=True)
        if m == 0:
            dgain_ref[...] = piece
        else:
            dgain_ref[...] += piece

    g_all = g_keep[...].reshape(micros * rows, width)
    for c in range(0, width, 256):
        dout_ref[:, c:c + 256] = dot_tn(a_keep[...], g_all[:, c:c + 256])
    for c in range(0, 3 * width, 256):
        dqkv_ref[:, c:c + 256] = dot_tn(n_keep[...], dp_keep[:, c:c + 256])

    for m in range(micros):
        @pl.when(jnp.logical_not(last))
        def _():
            fwd_copy(m).wait_send()

        @pl.when(jnp.logical_not(first))
        def _():
            bwd_copy(m).wait_send()


def per_device(tokens, cotangent, window_slot, slot_token, norm_gain, qkv_weight, out_weight):
    micros, rows, width = tokens.shape
    sections = lax.axis_size("section")
    send_order = jnp.argsort(window_slot // rows, stable=True)
    slot_place = jnp.argsort(jnp.argsort(slot_token))
    both = jnp.concatenate([tokens, cotangent], axis=0).transpose(1, 0, 2).reshape(rows, -1)
    both = lax.all_to_all(
        jnp.take(both, send_order, axis=0), "tok", split_axis=0, concat_axis=0, tiled=True
    )
    both = jnp.take(both, slot_place, axis=0)
    enter = both.reshape(rows, 2 * micros, width).transpose(1, 0, 2)
    in_vmem = pl.BlockSpec(memory_space=pltpu.VMEM)
    dma = pltpu.SemaphoreType.DMA((micros,))
    qkv_total, out_total, gain_total = pl.pallas_call(
        functools.partial(chain_kernel, sections, micros),
        out_shape=(
            jax.ShapeDtypeStruct((width, 3 * width), F32),
            jax.ShapeDtypeStruct((width, width), F32),
            jax.ShapeDtypeStruct((1, width), F32),
        ),
        in_specs=[in_vmem] * 4,
        out_specs=[in_vmem] * 3,
        scratch_shapes=[
            pltpu.VMEM((micros, rows, width), BF16),
            pltpu.VMEM((micros, rows, width), BF16),
            pltpu.VMEM((micros * rows, width), BF16),
            pltpu.VMEM((micros * rows, width), BF16),
            pltpu.VMEM((micros, rows, 3 * width), BF16),
            pltpu.VMEM((micros, width // PAIR, 2 * rows, rows), F32),
            pltpu.VMEM((micros * rows, 3 * width), BF16),
            pltpu.VMEM((micros, rows, width), BF16),
            pltpu.VMEM((micros, rows, width), BF16),
            dma, dma, dma, dma,
        ],
        compiler_params=pltpu.CompilerParams(
            collective_id=0, has_side_effects=True, vmem_limit_bytes=50 * 2**20
        ),
        name="chain",
    )(enter, norm_gain, qkv_weight[0], out_weight[0])
    qkv_share = lax.psum_scatter(qkv_total, "tok", scatter_dimension=0, tiled=True)
    out_share = lax.psum_scatter(out_total, "tok", scatter_dimension=0, tiled=True)
    gain_share = lax.psum_scatter(gain_total[0], "tok", scatter_dimension=0, tiled=True)
    return (qkv_share[None], out_share[None], gain_share[None])


def solution(mesh):
    placed = (
        P(None, "tok", None),
        P(None, "tok", None),
        P("tok"),
        P("tok"),
        P("section", None),
        P("section", None, None),
        P("section", None, None),
    )
    return jax.shard_map(
        per_device,
        mesh=mesh,
        in_specs=placed,
        out_specs=(P("section", "tok", None), P("section", "tok", None), P("section", "tok")),
        check_vma=False,
    )
```

time: 567 us -> 236 us (0.42)
  local copies, waits for them, and re-layouts: 176 us -> 4.44 us
  matrix products: 151 us -> 0 us
  Pallas kernels: 0 us -> 70.6 us
  other arithmetic: 50.2 us -> 10.7 us
  starting transfers between devices: 29 us -> 6.42 us
  waiting for transfers between devices: 119 us -> 110 us
    dot_general x60 -> x0, matrix products: 125 us -> none  [the longest x5 35.2 us: backward_step(): jnp.einsum('td,tc->dc', kept_rows, grad_proj, preferred_element_type=jnp....]
    pallas_call x0 -> x1, Pallas kernels: none -> 70.6 us  [per_device(): pl.pallas_call(functools.partial(chain_kernel, sections, micros), out_sha...]
    convert_element_type x25 -> x0, local copies, waits for them, and re-layouts: 53 us -> none  [the longest x15 30.4 us: window_forward(): return mixed_rows.reshape(window_rows.shape[0], -1).astype(jnp.bfloat16)]
    reshape x17 -> x2, local copies, waits for them, and re-layouts: 38.8 us -> 0.38 us  [the longest x1 0.3 us: per_device(): enter = both.reshape(rows, 2 * micros, width).transpose(1, 0, 2)]
    dynamic_slice x20 -> x0, local copies, waits for them, and re-layouts: 28.6 us -> none  [the longest x15 19 us: stored_update(): former = lax.dynamic_index_in_dim(stored, position, 0, keepdims=False)]
    sub x10 -> x0, matrix products: 26.8 us -> none  [window_soft(): return jax.nn.softmax(scores, axis=-1)]
    slice x11 -> x0, local copies, waits for them, and re-layouts: 26.5 us -> none  [the longest x10 25.5 us: window_split(): return (shaped[:, :, 0], shaped[:, :, 1], shaped[:, :, 2], head_dim)]
    ppermute x10 -> x0, starting transfers between devices: 22.6 us -> none  [from_behind(): lax.ppermute(value, axis, [(source, source + steps) for source in range(f...]
  transfers between devices with their start and end apart: 13 -> 3, of which waited for: 3 -> 3; matrix products, arithmetic and copies ran while one was open for 13% -> 3% of each run, Pallas kernels for 0% -> 0%
where the time goes in v2:
time: 236 us; the launch traced here: 233 us
  waiting for transfers between devices  110 us (47%)
  Pallas kernels  70.6 us (30%)
  blocking collectives  16 us (7%)
  between operations  14.8 us (6%)
  other arithmetic  10.7 us (5%)
  starting transfers between devices  6.42 us (3%)
  local copies, waits for them, and re-layouts  4.44 us (2%)
    reduce_scatter x1, waiting for transfers between devices, per_device(): lax.psum_scatter(qkv_total, 'tok', scatter_dimension=0, tiled=True)  79.1 us
    pallas_call x1, Pallas kernels, per_device(): pl.pallas_call(functools.partial(chain_kernel, sections, micros), out_sha...  70.6 us
    unnamed x1, blocking collectives  16 us
    reduce_scatter x1, waiting for transfers between devices, per_device(): lax.psum_scatter(out_total, 'tok', scatter_dimension=0, tiled=True)  15.6 us
    all_to_all x1, waiting for transfers between devices, per_device(): lax.all_to_all(jnp.take(both, send_order, axis=0), 'tok', split_axis=0, c...  15 us
    all_to_all x1, starting transfers between devices, per_device(): lax.all_to_all(jnp.take(both, send_order, axis=0), 'tok', split_axis=0, c...  6.38 us
    sort x2, other arithmetic, per_device(): slot_place = jnp.argsort(jnp.argsort(slot_token))  5.07 us
  transfers between devices with their start and end apart: 3, of which 3 were waited for; matrix products, arithmetic and copies ran while one was open for 3% of the time, Pallas kernels for 0%

profile of v2, /device:TPU:1, one launch (start us, length us, event | category | flops | bytes accessed | tf_op | source)
XLA Modules:
  0.0 233.3 jit_solution(10438870793877395055)
XLA Ops:
  7.2 0.7 and_select_fusion
  7.8 2.5 %sort.48 = (s32[128]{0:T(128)}, s32[128]{0:T(128)S(1)}) sort(s32[128]{0:T(128)S(1)} %and_select_fusion, s32[128]{0:T(128)S(1)} %iota.11), dimensions={0}, to_apply=%region_0.1 | sort | flops 896 | bytes 2048 | tf_op jit(solution)/shard_map/jit(argsort)/sort | solution.py:196
  10.4 1.2 maximum_bitcast_fusion
  11.6 0.1 copy.17
  11.7 0.0 copy-start.2
  11.7 1.0 gather_fusion
  12.7 1.0 broadcast_select_fusion.1
  13.7 6.4 %all-to-all-start = ((bf16[8,16,3072]{2,1,0:T(8,128)(2,1)}), bf16[8,16,3072]{2,1,0:T(8,128)(2,1)S(1)}, u32[]{:S(2)}, u32[]{:S(2)}) async-start(bf16[8,16,3072]{2,1,0:T(8,128)(2,1)} %bitcast.1), calls=%async_computation | async-start | bytes 1572864 | tf_op jit(solution)/shard_map/all_to_all | solution.py:199
  20.1 0.0 reduce-scatter.5.cloned.1.call-start
  20.1 0.0 copy-done.2
  20.1 2.5 %sort.49 = (s32[128]{0:T(128)}, s32[128]{0:T(128)S(1)}) sort(s32[128]{0:T(128)S(1)} %copy-done.2, s32[128]{0:T(128)S(1)} %iota.12), dimensions={0}, to_apply=%region_1.3 | sort | flops 896 | bytes 2048 | tf_op jit(solution)/shard_map/jit(argsort)/sort | solution.py:197
  22.7 2.5 %sort.50 = (s32[128]{0:T(128)}, s32[128]{0:T(128)S(1)}) sort(s32[128]{0:T(128)S(1)} %get-tuple-element.11, s32[128]{0:T(128)S(1)} %iota.13), dimensions={0}, to_apply=%region_2.4 | sort | flops 896 | bytes 2048 | tf_op jit(solution)/shard_map/jit(argsort)/sort | solution.py:197
  25.2 15.0 %all-to-all-done = bf16[8,16,3072]{2,1,0:T(8,128)(2,1)S(1)} async-done(((bf16[8,16,3072]{2,1,0:T(8,128)(2,1)}), bf16[8,16,3072]{2,1,0:T(8,128)(2,1)S(1)}, u32[]{:S(2)}, u32[]{:S(2)}) %all-to-all-start) | async-done | bytes 786464 | tf_op jit(solution)/shard_map/all_to_all | solution.py:199
  40.2 1.0 gather_fusion.1
  41.3 0.0 copy-start
  41.3 0.0 copy-start.1
  41.3 0.1 broadcast_select_fusion
  41.4 0.4 copy.15
  41.8 0.3 copy.16
  42.1 0.4 copy-done
  42.5 0.0 copy-done.1
  42.6 70.6 %chain.1 = (f32[768,2304]{1,0:T(8,128)}, f32[768,768]{1,0:T(8,128)}, f32[1,768]{1,0:T(1,128)S(1)}) custom-call(bf16[4,128,768]{2,1,0:T(8,128)(2,1)S(1)} %bitcast.15, f32[1,768]{1,0:T(1,128)S(1)} %copy-done.1, bf16[768,2304]{1,0:T(8,128)(2,1)} %bitcast.19, bf16[768,768]{1,0:T(8,128)(2,1)S(1)} %bitcast.16), custom_call_target="tpu_custom_call" | custom-call | tf_op jit(solution)/shard_map/chain/pallas_call | solution.py:206
  113.2 0.0 reduce-scatter.5.cloned.1.call-update
  113.2 0.0 reduce-scatter.3.cloned.1.call-start
  113.3 0.0 copy-start.3
  113.3 0.7 reduce-scatter.3.cloned.1.call-update
  114.0 0.0 copy-done.3
  114.0 0.6 dynamic-slice
  115.2 16.0 %all-reduce = f32[768]{0:T(1024)S(1)} all-reduce(f32[768]{0:T(1024)S(1)} %reduce), channel_id=4, replica_groups=mesh['section'=4,'tok'=8] {'tok'}, use_global_device_ids=true, to_apply=%region_5.7.clone | all-reduce | flops 768 | bytes 6144
  131.2 0.6 dynamic-slice_bitcast_fusion
  131.8 15.6 %reduce-scatter.5.cloned.1.call-done = f32[96,768]{1,0:T(8,128)} async-done(((f32[768,768]{1,0:T(8,128)}), f32[96,768]{1,0:T(8,128)}) %reduce-scatter.5.cloned.1.call-update) | async-done | bytes 294928 | tf_op jit(solution)/shard_map/reduce_scatter | solution.py:233
  147.4 79.1 %reduce-scatter.3.cloned.1.call-done = f32[96,2304]{1,0:T(8,128)} async-done(((f32[768,2304]{1,0:T(8,128)}), f32[96,2304]{1,0:T(8,128)}) %reduce-scatter.3.cloned.1.call-update) | async-done | bytes 884752 | tf_op jit(solution)/shard_map/reduce_scatter | solution.py:232
  (10 shorter events, 0.1 us)
Async XLA Ops:
  11.7 8.5 %copy-start.2 = (s32[128]{0:T(128)S(1)}, s32[128]{0:T(128)}, u32[]{:S(2)}) copy-start(s32[128]{0:T(128)} %param.12) | copy-start | bytes 1540
  13.7 26.5 %all-to-all-start = ((bf16[8,16,3072]{2,1,0:T(8,128)(2,1)}), bf16[8,16,3072]{2,1,0:T(8,128)(2,1)S(1)}, u32[]{:S(2)}, u32[]{:S(2)}) async-start(bf16[8,16,3072]{2,1,0:T(8,128)(2,1)} %bitcast.1), calls=%async_computation | async-start | bytes 1572864 | tf_op jit(solution)/shard_map/all_to_all | solution.py:199
  20.1 127.3 %reduce-scatter.5.cloned.1.call-start = ((), (), s32[]{:S(2)}) async-start(), calls=%async_computation.4 | async-start | bytes 2654208 | tf_op jit(solution)/shard_map/reduce_scatter | solution.py:233
  41.3 1.3 copy-start
  41.3 1.3 copy-start.1
  113.2 113.3 %reduce-scatter.3.cloned.1.call-start = ((), (), s32[]{:S(2)}) async-start(), calls=%async_computation.3 | async-start | bytes 7962624 | tf_op jit(solution)/shard_map/reduce_scatter | solution.py:232
  113.3 0.7 copy-start.3
Sparse Core Ops, SparseCore 0:
  113.3 34.0 reduce-scatter.4
  150.3 76.1 reduce-scatter.2

commit v3 on v2

--- a/solution.py
+++ b/solution.py
@@ -39,10 +39,10 @@
 
 
 def chain_kernel(
-    sections, micros, enter_ref, gain_ref, wqkv_ref, wout_ref,
+    sections, toks, micros, reduce_here, enter_ref, gain_ref, wqkv_ref, wout_ref,
     dqkv_ref, dout_ref, dgain_ref,
     x_keep, g_keep, n_keep, a_keep, qkv_keep, p_keep, dp_keep, xbox, gbox,
-    fwd_send, fwd_recv, bwd_send, bwd_recv,
+    fwd_send, fwd_recv, bwd_send, bwd_recv, *reduce_refs,
 ):
     rows, width = enter_ref.shape[1], enter_ref.shape[2]
     head_dim = width // HEADS
@@ -51,25 +51,24 @@
     first, last = here == 0, here == sections - 1
     barrier = pltpu.get_barrier_semaphore()
 
-    @pl.when(jnp.logical_not(first))
-    def _():
-        pl.semaphore_signal(barrier, inc=1, device_id={"section": here - 1},
-                            device_id_type=pl.DeviceIdType.MESH)
-
-    @pl.when(jnp.logical_not(last))
-    def _():
-        pl.semaphore_signal(barrier, inc=1, device_id={"section": here + 1},
-                            device_id_type=pl.DeviceIdType.MESH)
-
-    middle = jnp.logical_not(jnp.logical_or(first, last))
-
-    @pl.when(middle)
-    def _():
-        pl.semaphore_wait(barrier, 2)
-
-    @pl.when(jnp.logical_not(middle))
-    def _():
-        pl.semaphore_wait(barrier, 1)
+    def greet(condition, **peer):
+        @pl.when(condition)
+        def _():
+            pl.semaphore_signal(barrier, inc=1, device_id=peer,
+                                device_id_type=pl.DeviceIdType.MESH)
+
+    greet(jnp.logical_not(first), section=here - 1)
+    greet(jnp.logical_not(last), section=here + 1)
+    peers = jnp.where(first, 0, 1) + jnp.where(last, 0, 1)
+    if reduce_here:
+        tok_at = lax.axis_index("tok")
+        depth, core = tok_at // 2, tok_at % 2
+        depths = toks // 2
+        greet(depth > 0, tok=tok_at - 2)
+        greet(depth < depths - 1, tok=tok_at + 2)
+        greet(depth >= 0, tok=tok_at + 1 - 2 * core)
+        peers = peers + 1 + jnp.where(depth > 0, 1, 0) + jnp.where(depth < depths - 1, 1, 0)
+    pl.semaphore_wait(barrier, peers)
 
     gain = gain_ref[...]
     lane = lax.broadcasted_iota(jnp.int32, (1, PAIR), 1)
@@ -169,16 +168,113 @@
             bwd_copy(m).start()
 
         piece = jnp.sum(grad_normed * x * factor, axis=0, keepdims=True)
-        if m == 0:
-            dgain_ref[...] = piece
-        else:
-            dgain_ref[...] += piece
+        gain_total = piece if m == 0 else gain_total + piece
 
     g_all = g_keep[...].reshape(micros * rows, width)
+    if reduce_here:
+        (total, core_send, core_recv, up_send, up_recv, down_send, down_recv,
+         core_ss, core_rs, up_ss, up_rs, down_ss, down_rs) = reduce_refs
+        total_qkv, total_out = total.at[:, :3 * width], total.at[:, 3 * width:4 * width]
+        total[:, 4 * width:] = jnp.transpose(jnp.broadcast_to(gain_total, (PAIR, width)))
+    else:
+        total_qkv, total_out = dqkv_ref, dout_ref
+        dgain_ref[...] = gain_total
     for c in range(0, width, 256):
-        dout_ref[:, c:c + 256] = dot_tn(a_keep[...], g_all[:, c:c + 256])
+        total_out[:, c:c + 256] = dot_tn(a_keep[...], g_all[:, c:c + 256])
     for c in range(0, 3 * width, 256):
-        dqkv_ref[:, c:c + 256] = dot_tn(n_keep[...], dp_keep[:, c:c + 256])
+        total_qkv[:, c:c + 256] = dot_tn(n_keep[...], dp_keep[:, c:c + 256])
+
+    if reduce_here:
+        share = width // toks
+        order = []
+        for i in range(depths):
+            for d in (depths - 1 - i, i):
+                if d not in order:
+                    order.append(d)
+
+        def part(d, c):
+            return total[pl.ds(pl.multiple_of((2 * d + c) * share, share), share), :]
+
+        def to_tok(src, dst, send, recv, tok):
+            return pltpu.make_async_remote_copy(
+                src_ref=src, dst_ref=dst, send_sem=send, recv_sem=recv,
+                device_id={"tok": tok}, device_id_type=pl.DeviceIdType.MESH,
+            )
+
+        def core_copy(d):
+            return to_tok(core_send.at[d], core_recv.at[d], core_ss.at[d], core_rs.at[d],
+                          tok_at + 1 - 2 * core)
+
+        def up_copy(d):
+            return to_tok(up_send.at[d], up_recv.at[d], up_ss.at[d], up_rs.at[d], tok_at + 2)
+
+        def down_copy(d):
+            return to_tok(down_send.at[d], down_recv.at[d], down_ss.at[d], down_rs.at[d],
+                          tok_at - 2)
+
+        for d in order:
+            core_send[d] = part(d, 1 - core).astype(BF16)
+            core_copy(d).start()
+
+        def pass_up(d):
+            @pl.when(depth == 0)
+            def _():
+                up_send[d] = (part(d, core) + core_recv[d].astype(F32)).astype(BF16)
+
+            @pl.when(depth > 0)
+            def _():
+                up_copy(d).wait_recv()
+                up_send[d] = (part(d, core) + core_recv[d].astype(F32)
+                              + up_recv[d].astype(F32)).astype(BF16)
+
+            up_copy(d).start()
+
+        def pass_down(d):
+            @pl.when(depth == depths - 1)
+            def _():
+                down_send[d] = (part(d, core) + core_recv[d].astype(F32)).astype(BF16)
+
+            @pl.when(depth < depths - 1)
+            def _():
+                down_copy(d).wait_recv()
+                down_send[d] = (part(d, core) + core_recv[d].astype(F32)
+                                + down_recv[d].astype(F32)).astype(BF16)
+
+            down_copy(d).start()
+
+        waited = []
+        for i in range(depths):
+            for d in (depths - 1 - i, i):
+                if d not in waited:
+                    core_copy(d).wait_recv()
+                    waited.append(d)
+            if i < depths - 1:
+                pl.when(depth < depths - 1 - i)(functools.partial(pass_up, depths - 1 - i))
+                pl.when(depth > i)(functools.partial(pass_down, i))
+
+        for d in range(depths):
+            @pl.when(depth == d)
+            def _():
+                mine = part(d, core) + core_recv[d].astype(F32)
+                if d > 0:
+                    up_copy(d).wait_recv()
+                    mine = mine + up_recv[d].astype(F32)
+                if d < depths - 1:
+                    down_copy(d).wait_recv()
+                    mine = mine + down_recv[d].astype(F32)
+                dqkv_ref[...] = mine[:, :3 * width]
+                dout_ref[...] = mine[:, 3 * width:4 * width]
+                dgain_ref[...] = mine[:, 4 * width:]
+
+            core_copy(d).wait_send()
+
+            @pl.when(depth < d)
+            def _():
+                up_copy(d).wait_send()
+
+            @pl.when(depth > d)
+            def _():
+                down_copy(d).wait_send()
 
     for m in range(micros):
         @pl.when(jnp.logical_not(last))
@@ -193,8 +289,14 @@
 def per_device(tokens, cotangent, window_slot, slot_token, norm_gain, qkv_weight, out_weight):
     micros, rows, width = tokens.shape
     sections = lax.axis_size("section")
-    send_order = jnp.argsort(window_slot // rows, stable=True)
-    slot_place = jnp.argsort(jnp.argsort(slot_token))
+    toks = lax.axis_size("tok")
+    share = width // toks
+    reduce_here = toks % 2 == 0 and toks >= 4 and share % 16 == 0 and width % toks == 0
+    place = jnp.arange(rows, dtype=jnp.int32)
+    target = (window_slot // rows) * rows + place
+    send_rank = jnp.sum((target[None, :] < target[:, None]).astype(jnp.int32), axis=1)
+    send_order = jnp.sum(jnp.where(send_rank[None, :] == place[:, None], place[None, :], 0), axis=1)
+    slot_place = jnp.sum((slot_token[None, :] < slot_token[:, None]).astype(jnp.int32), axis=1)
     both = jnp.concatenate([tokens, cotangent], axis=0).transpose(1, 0, 2).reshape(rows, -1)
     both = lax.all_to_all(
         jnp.take(both, send_order, axis=0), "tok", split_axis=0, concat_axis=0, tiled=True
@@ -203,13 +305,25 @@
     enter = both.reshape(rows, 2 * micros, width).transpose(1, 0, 2)
     in_vmem = pl.BlockSpec(memory_space=pltpu.VMEM)
     dma = pltpu.SemaphoreType.DMA((micros,))
-    qkv_total, out_total, gain_total = pl.pallas_call(
-        functools.partial(chain_kernel, sections, micros),
-        out_shape=(
+    if reduce_here:
+        out_shape = (
+            jax.ShapeDtypeStruct((share, 3 * width), F32),
+            jax.ShapeDtypeStruct((share, width), F32),
+            jax.ShapeDtypeStruct((share, PAIR), F32),
+        )
+        box = pltpu.VMEM((toks // 2, share, 4 * width + PAIR), BF16)
+        extra = [pltpu.VMEM((width, 4 * width + PAIR), F32)] + [box] * 6
+        extra += [pltpu.SemaphoreType.DMA((toks // 2,))] * 6
+    else:
+        out_shape = (
             jax.ShapeDtypeStruct((width, 3 * width), F32),
             jax.ShapeDtypeStruct((width, width), F32),
             jax.ShapeDtypeStruct((1, width), F32),
-        ),
+        )
+        extra = []
+    qkv_total, out_total, gain_total = pl.pallas_call(
+        functools.partial(chain_kernel, sections, toks, micros, reduce_here),
+        out_shape=out_shape,
         in_specs=[in_vmem] * 4,
         out_specs=[in_vmem] * 3,
         scratch_shapes=[
@@ -223,12 +337,15 @@
             pltpu.VMEM((micros, rows, width), BF16),
             pltpu.VMEM((micros, rows, width), BF16),
             dma, dma, dma, dma,
+            *extra,
         ],
         compiler_params=pltpu.CompilerParams(
-            collective_id=0, has_side_effects=True, vmem_limit_bytes=50 * 2**20
+            collective_id=0, has_side_effects=True, vmem_limit_bytes=56 * 2**20
         ),
         name="chain",
     )(enter, norm_gain, qkv_weight[0], out_weight[0])
+    if reduce_here:
+        return (qkv_total[None], out_total[None], gain_total[:, 0][None])
     qkv_share = lax.psum_scatter(qkv_total, "tok", scatter_dimension=0, tiled=True)
     out_share = lax.psum_scatter(out_total, "tok", scatter_dimension=0, tiled=True)
     gain_share = lax.psum_scatter(gain_total[0], "tok", scatter_dimension=0, tiled=True)

time: 236 us -> 167 us (0.71)
  waiting for transfers between devices: 110 us -> 19.9 us
  Pallas kernels: 70.6 us -> 127 us
  blocking collectives: 16 us -> 0 us
  between operations: 14.8 us -> 0.75 us
  other arithmetic: 10.7 us -> 3.5 us
  local copies, waits for them, and re-layouts: 4.44 us -> 8.94 us
    reduce_scatter x2 -> x0, waiting for transfers between devices: 94.7 us -> none  [the longest x1 79.1 us: per_device(): lax.psum_scatter(qkv_total, 'tok', scatter_dimension=0, tiled=True)]
    pallas_call x1, Pallas kernels: 70.6 us -> 127 us  [per_device(): pl.pallas_call(functools.partial(chain_kernel, sections, toks, micros, re...]
    unnamed x1 -> x0, blocking collectives: 16 us -> none
    sort x3 -> x0, other arithmetic: 7.61 us -> none  [the longest x2 5.07 us: per_device(): slot_place = jnp.argsort(jnp.argsort(slot_token))]
    all_to_all x1, waiting for transfers between devices: 15 us -> 19.9 us  [per_device(): lax.all_to_all(jnp.take(both, send_order, axis=0), 'tok', split_axis=0, c...]
    unnamed x9 -> x4, local copies, waits for them, and re-layouts: 1.01 us -> 3.83 us
  transfers between devices with their start and end apart: 3 -> 1, of which waited for: 3 -> 1; matrix products, arithmetic and copies ran while one was open for 3% -> 0% of each run, Pallas kernels for 0% -> 0%
where the time goes in v3:
time: 167 us; the launch traced here: 166 us
  Pallas kernels  127 us (76%)
  waiting for transfers between devices  19.9 us (12%)
  local copies, waits for them, and re-layouts  8.94 us (5%)
  starting transfers between devices  6.38 us (4%)
  other arithmetic  3.5 us (2%)
    pallas_call x1, Pallas kernels, per_device(): pl.pallas_call(functools.partial(chain_kernel, sections, toks, micros, re...  127 us
    all_to_all x1, waiting for transfers between devices, per_device(): lax.all_to_all(jnp.take(both, send_order, axis=0), 'tok', split_axis=0, c...  19.9 us
    all_to_all x1, starting transfers between devices, per_device(): lax.all_to_all(jnp.take(both, send_order, axis=0), 'tok', split_axis=0, c...  6.38 us
    unnamed x4, local copies, waits for them, and re-layouts  3.83 us
  transfers between devices with their start and end apart: 1, of which 1 were waited for; matrix products, arithmetic and copies ran while one was open for 0% of the time, Pallas kernels for 0%

profile of v3, /device:TPU:1, one launch (start us, length us, event | category | flops | bytes accessed | tf_op | source)
XLA Modules:
  0.0 166.2 jit_solution(16974871309374406094)
XLA Ops:
  0.6 0.7 iota_add_fusion
  1.3 0.2 convert_reduce_fusion.1
  1.5 0.1 select_reduce_fusion
  1.6 1.2 maximum_bitcast_fusion
  2.8 0.1 copy.17
  2.9 0.0 copy-start
  2.9 1.0 gather_fusion
  4.0 1.0 broadcast_select_fusion.1
  5.0 6.4 %all-to-all-start = ((bf16[8,16,3072]{2,1,0:T(8,128)(2,1)}), bf16[8,16,3072]{2,1,0:T(8,128)(2,1)S(1)}, u32[]{:S(2)}, u32[]{:S(2)}) async-start(bf16[8,16,3072]{2,1,0:T(8,128)(2,1)} %bitcast.1), calls=%async_computation | async-start | bytes 1572864 | tf_op jit(solution)/shard_map/all_to_all | solution.py:301
  11.4 0.0 copy-done
  11.4 0.2 convert_reduce_fusion
  11.6 19.9 %all-to-all-done = bf16[8,16,3072]{2,1,0:T(8,128)(2,1)S(1)} async-done(((bf16[8,16,3072]{2,1,0:T(8,128)(2,1)}), bf16[8,16,3072]{2,1,0:T(8,128)(2,1)S(1)}, u32[]{:S(2)}, u32[]{:S(2)}) %all-to-all-start) | async-done | bytes 786464 | tf_op jit(solution)/shard_map/all_to_all | solution.py:301
  31.5 1.0 gather_fusion.1
  32.5 0.1 broadcast_select_fusion
  32.7 0.4 copy.15
  33.0 1.2 copy.16
  34.2 126.7 %chain.1 = (f32[96,2304]{1,0:T(8,128)}, f32[96,768]{1,0:T(8,128)}, f32[96,128]{1,0:T(8,128)}) custom-call(bf16[4,128,768]{2,1,0:T(8,128)(2,1)} %bitcast.17, f32[1,768]{1,0:T(1,128)} %gain_ref.1, bf16[768,2304]{1,0:T(8,128)(2,1)} %bitcast.15, bf16[768,768]{1,0:T(8,128)(2,1)} %bitcast.18), custom_call_target="tpu_custom_call" | custom-call | tf_op jit(solution)/shard_map/chain/pallas_call | solution.py:324
  160.9 1.4 slice_reduce_fusion
  162.4 2.1 %copy.20 = f32[1,96,2304]{2,1,0:T(8,128)} copy(f32[1,96,2304]{2,1,0:T(8,128)} %bitcast.19) | data formatting | bytes 1769472
  164.5 1.7 %copy.21 = f32[1,96,768]{2,1,0:T(8,128)} copy(f32[1,96,768]{2,1,0:T(8,128)} %bitcast.20) | data formatting | bytes 589824
  (6 shorter events, 0.0 us)
Async XLA Ops:
  2.9 8.5 %copy-start = (s32[128]{0:T(128)S(1)}, s32[128]{0:T(128)}, u32[]{:S(2)}) copy-start(s32[128]{0:T(128)} %param.12) | copy-start | bytes 1540
  5.0 26.5 %all-to-all-start = ((bf16[8,16,3072]{2,1,0:T(8,128)(2,1)}), bf16[8,16,3072]{2,1,0:T(8,128)(2,1)S(1)}, u32[]{:S(2)}, u32[]{:S(2)}) async-start(bf16[8,16,3072]{2,1,0:T(8,128)(2,1)} %bitcast.1), calls=%async_computation | async-start | bytes 1572864 | tf_op jit(solution)/shard_map/all_to_all | solution.py:301

commit v4 on v3

--- a/solution.py
+++ b/solution.py
@@ -39,12 +39,13 @@
 
 
 def chain_kernel(
-    sections, toks, micros, reduce_here, enter_ref, gain_ref, wqkv_ref, wout_ref,
+    sections, toks, micros, reduce_here, enter_ref, leave_ref, send_ref, place_ref, gain_ref, wqkv_ref, wout_ref,
     dqkv_ref, dout_ref, dgain_ref,
     x_keep, g_keep, n_keep, a_keep, qkv_keep, p_keep, dp_keep, xbox, gbox,
     fwd_send, fwd_recv, bwd_send, bwd_recv, *reduce_refs,
 ):
     rows, width = enter_ref.shape[1], enter_ref.shape[2]
+    share = width // toks
     head_dim = width // HEADS
     temper = head_dim ** (-0.5)
     here = lax.axis_index("section")
@@ -64,10 +65,9 @@
         tok_at = lax.axis_index("tok")
         depth, core = tok_at // 2, tok_at % 2
         depths = toks // 2
-        greet(depth > 0, tok=tok_at - 2)
-        greet(depth < depths - 1, tok=tok_at + 2)
-        greet(depth >= 0, tok=tok_at + 1 - 2 * core)
-        peers = peers + 1 + jnp.where(depth > 0, 1, 0) + jnp.where(depth < depths - 1, 1, 0)
+        for o in range(1, toks):
+            greet(depth >= 0, tok=(tok_at + o) % toks)
+        peers = peers + (toks - 1)
     pl.semaphore_wait(barrier, peers)
 
     gain = gain_ref[...]
@@ -79,6 +79,50 @@
     hide = jnp.where(row_window == col_window, 0.0, -1e30)
     hide = jnp.concatenate([hide, hide], axis=0)
 
+    if reduce_here:
+        (total, core_send, core_recv, up_send, up_recv, down_send, down_recv,
+         core_ss, core_rs, up_ss, up_rs, down_ss, down_rs,
+         packed, landed, packed_ss, packed_rs) = reduce_refs
+        outer = jnp.logical_or(first, last)
+        block = rows // toks
+
+        def rows_of(index):
+            return pl.ds(pl.multiple_of(index * block, block), block)
+
+        def shuffle_copy(o):
+            return pltpu.make_async_remote_copy(
+                src_ref=packed.at[:, rows_of((tok_at + o) % toks), :],
+                dst_ref=landed.at[:, rows_of(tok_at), :],
+                send_sem=packed_ss.at[o], recv_sem=packed_rs.at[o],
+                device_id={"tok": (tok_at + o) % toks}, device_id_type=pl.DeviceIdType.MESH,
+            )
+
+        def pack(source_ref):
+            spot = lax.broadcasted_iota(jnp.int32, (rows, rows), 0)
+            pick = jnp.where(spot == send_ref[...], 1.0, 0.0).astype(BF16)
+            for m in range(micros):
+                packed[m] = dot_nn(pick, source_ref[m]).astype(BF16)
+
+        def unpack(target_ref):
+            spot = lax.broadcasted_iota(jnp.int32, (rows, rows), 1)
+            pick = jnp.where(spot == place_ref[...], 1.0, 0.0).astype(BF16)
+            for m in range(micros):
+                target_ref[m] = dot_nn(pick, landed[m]).astype(BF16)
+
+        pl.when(first)(lambda: pack(enter_ref))
+        pl.when(last)(lambda: pack(leave_ref))
+
+        @pl.when(outer)
+        def _():
+            for o in range(1, toks):
+                shuffle_copy(o).start()
+            landed[:, rows_of(tok_at), :] = packed[:, rows_of(tok_at), :]
+            for o in range(1, toks):
+                shuffle_copy(o).wait()
+
+        pl.when(first)(lambda: unpack(x_keep))
+        pl.when(last)(lambda: unpack(g_keep))
+
     def two(value):
         return jnp.concatenate([value * low, value * high], axis=0)
 
@@ -97,9 +141,10 @@
     for m in range(micros):
         span = slice(m * rows, (m + 1) * rows)
 
-        @pl.when(first)
-        def _():
-            x_keep[m] = enter_ref[m]
+        if not reduce_here:
+            @pl.when(first)
+            def _():
+                x_keep[m] = enter_ref[m]
 
         @pl.when(jnp.logical_not(first))
         def _():
@@ -131,9 +176,10 @@
     for m in range(micros):
         span = slice(m * rows, (m + 1) * rows)
 
-        @pl.when(last)
-        def _():
-            g_keep[m] = enter_ref[micros + m]
+        if not reduce_here:
+            @pl.when(last)
+            def _():
+                g_keep[m] = leave_ref[m]
 
         @pl.when(jnp.logical_not(last))
         def _():
@@ -172,8 +218,6 @@
 
     g_all = g_keep[...].reshape(micros * rows, width)
     if reduce_here:
-        (total, core_send, core_recv, up_send, up_recv, down_send, down_recv,
-         core_ss, core_rs, up_ss, up_rs, down_ss, down_rs) = reduce_refs
         total_qkv, total_out = total.at[:, :3 * width], total.at[:, 3 * width:4 * width]
         total[:, 4 * width:] = jnp.transpose(jnp.broadcast_to(gain_total, (PAIR, width)))
     else:
@@ -185,7 +229,6 @@
         total_qkv[:, c:c + 256] = dot_tn(n_keep[...], dp_keep[:, c:c + 256])
 
     if reduce_here:
-        share = width // toks
         order = []
         for i in range(depths):
             for d in (depths - 1 - i, i):
@@ -292,17 +335,23 @@
     toks = lax.axis_size("tok")
     share = width // toks
     reduce_here = toks % 2 == 0 and toks >= 4 and share % 16 == 0 and width % toks == 0
+    reduce_here = reduce_here and rows % (16 * toks) == 0
     place = jnp.arange(rows, dtype=jnp.int32)
     target = (window_slot // rows) * rows + place
     send_rank = jnp.sum((target[None, :] < target[:, None]).astype(jnp.int32), axis=1)
-    send_order = jnp.sum(jnp.where(send_rank[None, :] == place[:, None], place[None, :], 0), axis=1)
     slot_place = jnp.sum((slot_token[None, :] < slot_token[:, None]).astype(jnp.int32), axis=1)
-    both = jnp.concatenate([tokens, cotangent], axis=0).transpose(1, 0, 2).reshape(rows, -1)
-    both = lax.all_to_all(
-        jnp.take(both, send_order, axis=0), "tok", split_axis=0, concat_axis=0, tiled=True
-    )
-    both = jnp.take(both, slot_place, axis=0)
-    enter = both.reshape(rows, 2 * micros, width).transpose(1, 0, 2)
+    enter, leave = tokens, cotangent
+    if not reduce_here:
+        send_order = jnp.sum(
+            jnp.where(send_rank[None, :] == place[:, None], place[None, :], 0), axis=1
+        )
+        both = jnp.concatenate([tokens, cotangent], axis=0).transpose(1, 0, 2).reshape(rows, -1)
+        both = lax.all_to_all(
+            jnp.take(both, send_order, axis=0), "tok", split_axis=0, concat_axis=0, tiled=True
+        )
+        both = jnp.take(both, slot_place, axis=0)
+        both = both.reshape(rows, 2 * micros, width).transpose(1, 0, 2)
+        enter, leave = both[:micros], both[micros:]
     in_vmem = pl.BlockSpec(memory_space=pltpu.VMEM)
     dma = pltpu.SemaphoreType.DMA((micros,))
     if reduce_here:
@@ -314,6 +363,8 @@
         box = pltpu.VMEM((toks // 2, share, 4 * width + PAIR), BF16)
         extra = [pltpu.VMEM((width, 4 * width + PAIR), F32)] + [box] * 6
         extra += [pltpu.SemaphoreType.DMA((toks // 2,))] * 6
+        extra += [pltpu.VMEM((micros, rows, width), BF16)] * 2
+        extra += [pltpu.SemaphoreType.DMA((toks,))] * 2
     else:
         out_shape = (
             jax.ShapeDtypeStruct((width, 3 * width), F32),
@@ -324,7 +375,7 @@
     qkv_total, out_total, gain_total = pl.pallas_call(
         functools.partial(chain_kernel, sections, toks, micros, reduce_here),
         out_shape=out_shape,
-        in_specs=[in_vmem] * 4,
+        in_specs=[in_vmem] * 7,
         out_specs=[in_vmem] * 3,
         scratch_shapes=[
             pltpu.VMEM((micros, rows, width), BF16),
@@ -343,7 +394,7 @@
             collective_id=0, has_side_effects=True, vmem_limit_bytes=56 * 2**20
         ),
         name="chain",
-    )(enter, norm_gain, qkv_weight[0], out_weight[0])
+    )(enter, leave, send_rank[None], slot_place[:, None], norm_gain, qkv_weight[0], out_weight[0])
     if reduce_here:
         return (qkv_total[None], out_total[None], gain_total[:, 0][None])
     qkv_share = lax.psum_scatter(qkv_total, "tok", scatter_dimension=0, tiled=True)

time: 167 us -> 151 us (0.904)
  waiting for transfers between devices: 19.9 us -> 0 us
  Pallas kernels: 127 us -> 141 us
  starting transfers between devices: 6.38 us -> 0 us
  local copies, waits for them, and re-layouts: 8.94 us -> 6 us
    all_to_all x1 -> x0, waiting for transfers between devices: 19.9 us -> none  [per_device(): lax.all_to_all(jnp.take(both, send_order, axis=0), 'tok', split_axis=0, c...]
    pallas_call x1, Pallas kernels: 127 us -> 141 us  [per_device(): pl.pallas_call(functools.partial(chain_kernel, sections, toks, micros, re...]
    all_to_all x1 -> x0, starting transfers between devices: 6.38 us -> none  [per_device(): lax.all_to_all(jnp.take(both, send_order, axis=0), 'tok', split_axis=0, c...]
    gather x2 -> x0, local copies, waits for them, and re-layouts: 2.06 us -> none  [the longest x1 1.03 us: per_device(): jnp.take(both, send_order, axis=0)]
    unnamed x4 -> x2, local copies, waits for them, and re-layouts: 3.83 us -> 3.83 us
  transfers between devices with their start and end apart: 1 -> 0, of which waited for: 1 -> 0; matrix products, arithmetic and copies ran while one was open for 0% -> 0% of each run, Pallas kernels for 0% -> 0%
where the time goes in v4:
time: 151 us; the launch traced here: 150 us
  Pallas kernels  141 us (93%)
  local copies, waits for them, and re-layouts  6 us (4%)
  other arithmetic  2.26 us (1%)
    pallas_call x1, Pallas kernels, per_device(): pl.pallas_call(functools.partial(chain_kernel, sections, toks, micros, re...  141 us
    unnamed x2, local copies, waits for them, and re-layouts  3.83 us

profile of v4, /device:TPU:1, one launch (start us, length us, event | category | flops | bytes accessed | tf_op | source)
XLA Modules:
  0.0 150.4 jit_solution(16574267656154730342)
XLA Ops:
  0.6 0.7 iota_add_fusion
  1.3 0.7 convert_reduce_fusion.1
  2.0 0.9 convert_reduce_fusion
  2.9 0.8 copy.12.place_ref
  3.6 141.5 %chain.1 = (f32[96,2304]{1,0:T(8,128)}, f32[96,768]{1,0:T(8,128)}, f32[96,128]{1,0:T(8,128)}) custom-call(bf16[2,128,768]{2,1,0:T(8,128)(2,1)} %enter_ref.1, bf16[2,128,768]{2,1,0:T(8,128)(2,1)} %leave_ref.1, s32[1,128]{1,0:T(1,128)} %bitcast.12, s32[128,1]{1,0:T(8,128)} %copy.12.place_ref, f32[1,768]{1,0:T(1,128)} %gain_ref.1, bf16[768,2304]{1,0:T(8,128)(2,1)} %bitcast.7, ...), custom_call_target="tpu_custom_call" | custom-call | tf_op jit(solution)/shard_map/chain/pallas_call | solution.py:375
  145.1 1.4 slice_reduce_fusion
  146.6 2.1 %copy.15 = f32[1,96,2304]{2,1,0:T(8,128)} copy(f32[1,96,2304]{2,1,0:T(8,128)} %bitcast.9) | data formatting | bytes 1769472
  148.7 1.7 %copy.16 = f32[1,96,768]{2,1,0:T(8,128)} copy(f32[1,96,768]{2,1,0:T(8,128)} %bitcast.10) | data formatting | bytes 589824

commit v5 on v4

--- a/solution.py
+++ b/solution.py
@@ -118,7 +118,7 @@
                 shuffle_copy(o).start()
             landed[:, rows_of(tok_at), :] = packed[:, rows_of(tok_at), :]
             for o in range(1, toks):
-                shuffle_copy(o).wait()
+                shuffle_copy(o).wait_recv()
 
         pl.when(first)(lambda: unpack(x_keep))
         pl.when(last)(lambda: unpack(g_keep))
@@ -163,7 +163,7 @@
             scores = dot_nt(two(q), k) * temper + hide
             top = jnp.max(scores, axis=-1, keepdims=True)
             raised = jnp.exp(scores - top)
-            soft = raised / jnp.sum(raised, axis=-1, keepdims=True)
+            soft = raised * (1.0 / jnp.sum(raised, axis=-1, keepdims=True))
             p_keep[m, j] = soft
             mixed = dot_nn(beside(soft.astype(BF16)), two(v))
             a_keep[span, c:c + PAIR] = mixed.astype(BF16)
@@ -318,6 +318,12 @@
             @pl.when(depth > d)
             def _():
                 down_copy(d).wait_send()
+
+    if reduce_here:
+        @pl.when(outer)
+        def _():
+            for o in range(1, toks):
+                shuffle_copy(o).wait_send()
 
     for m in range(micros):
         @pl.when(jnp.logical_not(last))

time: 151 us -> 151 us (level)
  no operation moved by 1% of the time
where the time goes in v5:
time: 151 us
  Pallas kernels  142 us (94%)
  local copies, waits for them, and re-layouts  6 us (4%)
  other arithmetic  2.26 us (1%)
    pallas_call x1, Pallas kernels, per_device(): pl.pallas_call(functools.partial(chain_kernel, sections, toks, micros, re...  142 us
    unnamed x2, local copies, waits for them, and re-layouts  3.83 us

profile of v5, /device:TPU:1, one launch (start us, length us, event | category | flops | bytes accessed | tf_op | source)
XLA Modules:
  0.0 150.5 jit_solution(10561667054530952513)
XLA Ops:
  0.6 0.7 iota_add_fusion
  1.3 0.7 convert_reduce_fusion.1
  2.0 0.9 convert_reduce_fusion
  2.9 0.8 copy.12.place_ref
  3.6 141.6 %chain.1 = (f32[96,2304]{1,0:T(8,128)}, f32[96,768]{1,0:T(8,128)}, f32[96,128]{1,0:T(8,128)}) custom-call(bf16[2,128,768]{2,1,0:T(8,128)(2,1)} %enter_ref.1, bf16[2,128,768]{2,1,0:T(8,128)(2,1)} %leave_ref.1, s32[1,128]{1,0:T(1,128)} %bitcast.12, s32[128,1]{1,0:T(8,128)} %copy.12.place_ref, f32[1,768]{1,0:T(1,128)} %gain_ref.1, bf16[768,2304]{1,0:T(8,128)(2,1)} %bitcast.7, ...), custom_call_target="tpu_custom_call" | custom-call | tf_op jit(solution)/shard_map/chain/pallas_call | solution.py:381
  145.3 1.4 slice_reduce_fusion
  146.7 2.1 %copy.15 = f32[1,96,2304]{2,1,0:T(8,128)} copy(f32[1,96,2304]{2,1,0:T(8,128)} %bitcast.9) | data formatting | bytes 1769472
  148.8 1.7 %copy.16 = f32[1,96,768]{2,1,0:T(8,128)} copy(f32[1,96,768]{2,1,0:T(8,128)} %bitcast.10) | data formatting | bytes 589824
